TPU v7x, 512 devices: a whole 4x8x8 slice. The times are simulated.
512 devices in a mesh: tm: 32 (over y_lo, z), tok: 16 (over y_hi, x, core).
Axes of the slice: x: 4, y: 8 (y_hi: 2, y_lo: 4; y = y_hi * 4 + y_lo), z: 8, core: 2. Of those that a mesh axis runs over, the one named last changes fastest.
Arguments:
- hidden_states: bfloat16 [32, 1024, 1280], P('tm', 'tok'), may hold values from -6 to 6
- norm_gain: float32 [1280], replicated, may hold values from 0.1 to 1.9
- norm_bias: float32 [1280], replicated, may hold values from -3 to 3
- q_weight: bfloat16 [1280, 1024], P(None, 'tok'), may hold values from -0.5 to 0.5
- k_weight: bfloat16 [1280, 1024], P(None, 'tok'), may hold values from -0.25 to 0.25
- v_weight: bfloat16 [1280, 1024], P(None, 'tok'), may hold values from -0.15625 to 0.15625
- out_weight: bfloat16 [1024, 1280], P('tok'), may hold values from -0.75 to 0.75
Outputs:
- attended_out: bfloat16 [32, 1024, 1280], P('tm', 'tok')
All inputs are finite; a program needn't handle non-finite values.
Results may differ from a plain program's by a relative error of at most 0.007.
The roundings to bfloat16 on the way count: a program that leaves them out, or rounds other values in their place, can miss the bound.
Values may be sent and summed in bfloat16 or wider, within the bound.
A program may use at most 64 MiB of HBM per device.

v0:
```python
import jax
import jax.numpy as jnp
from jax import lax
from jax.sharding import PartitionSpec as P

DH = 64


def broadcast(value, axis, source):
    kept = jnp.where(lax.axis_index(axis) == source, value, 0).astype(value.dtype)
    return lax.psum(kept, axis)


def passed_along(block, axis, distance):
    devices = range(lax.axis_size(axis))
    route = [(i - distance, i) for i in devices if i - distance in devices]
    return lax.ppermute(block, axis, route)


def layer_norm(states, norm_gain, norm_bias):
    widened = states.astype(jnp.float32)
    center = jnp.mean(widened, axis=-1, keepdims=True)
    spread = jnp.mean(jnp.square(widened - center), axis=-1, keepdims=True)
    scaled = (widened - center) * lax.rsqrt(spread + 1e-05)
    return (scaled * norm_gain + norm_bias).astype(jnp.bfloat16)


def attend_block(queries, anchor_keys, anchor_values, earlier_keys, earlier_values):
    scale = DH ** (-0.5)
    scores_anchor = (
        jnp.einsum("qhd,khd->hqk", queries, anchor_keys, preferred_element_type=jnp.float32) * scale
    )
    scores_prev = (
        jnp.einsum("qhd,khd->hqk", queries, earlier_keys, preferred_element_type=jnp.float32)
        * scale
    )
    highest = jnp.maximum(
        jnp.max(scores_anchor, axis=-1, keepdims=True), jnp.max(scores_prev, axis=-1, keepdims=True)
    )
    weights_anchor = jnp.exp(scores_anchor - highest)
    weights_prev = jnp.exp(scores_prev - highest)
    denominator = jnp.sum(weights_anchor, axis=-1, keepdims=True) + jnp.sum(
        weights_prev, axis=-1, keepdims=True
    )
    probs_anchor = (weights_anchor / denominator).astype(jnp.bfloat16)
    probs_prev = (weights_prev / denominator).astype(jnp.bfloat16)
    mixed = jnp.einsum(
        "hqk,khd->qhd", probs_anchor, anchor_values, preferred_element_type=jnp.float32
    )
    mixed = mixed + jnp.einsum(
        "hqk,khd->qhd", probs_prev, earlier_values, preferred_element_type=jnp.float32
    )
    return mixed.astype(jnp.bfloat16)


def body(hidden_states, norm_gain, norm_bias, q_weight, k_weight, v_weight, out_weight):
    frames, row_count, model_width = hidden_states.shape
    normed = layer_norm(hidden_states, norm_gain, norm_bias)
    stacked = jnp.stack((q_weight, k_weight, v_weight))
    flattened = normed.reshape(frames * row_count, model_width)
    projected = jnp.einsum(
        "td,nde->nte",
        flattened,
        lax.all_gather(stacked, "tok", axis=2, tiled=True),
        preferred_element_type=jnp.float32,
    ).astype(jnp.bfloat16)
    projected = projected.reshape(3, frames, row_count, projected.shape[2])
    packed = lax.all_to_all(projected, "tok", split_axis=3, concat_axis=2, tiled=True)
    frame_tokens = packed.shape[2]
    head_cols = packed.shape[3]
    heads_local = head_cols // DH
    queries = packed[0]
    keyval = packed[1:3]
    anchor = broadcast(keyval[:, 0], "tm", 0)
    incoming = passed_along(keyval[:, frames - 1], "tm", 1)
    at_start = lax.axis_index("tm") == 0
    incoming = jnp.where(at_start, keyval[:, 0], incoming)
    earlier = jnp.concatenate([incoming[:, None], keyval[:, : frames - 1]], axis=1)
    anchor_keys = anchor[0].reshape(frame_tokens, heads_local, DH)
    anchor_values = anchor[1].reshape(frame_tokens, heads_local, DH)
    block_rows = min(512, frame_tokens)
    block_count = frame_tokens // block_rows

    def one_frame(operands):
        query_frame, earlier_keys, earlier_values = operands
        earlier_keys = earlier_keys.reshape(frame_tokens, heads_local, DH)
        earlier_values = earlier_values.reshape(frame_tokens, heads_local, DH)
        query_blocks = query_frame.reshape(block_count, block_rows, heads_local, DH)

        def one_block(query_block):
            return attend_block(
                query_block, anchor_keys, anchor_values, earlier_keys, earlier_values
            )

        return lax.map(one_block, query_blocks).reshape(frame_tokens, head_cols)

    attended = lax.map(one_frame, (queries, earlier[0], earlier[1]))
    regathered = lax.all_to_all(attended, "tok", split_axis=1, concat_axis=2, tiled=True)
    mixed_rows = regathered.reshape(frames * row_count, regathered.shape[2])
    result = jnp.dot(
        mixed_rows,
        lax.all_gather(out_weight, "tok", axis=0, tiled=True),
        preferred_element_type=jnp.float32,
    )
    return result.astype(jnp.bfloat16).reshape(frames, row_count, model_width)


def solution(mesh):
    return jax.shard_map(
        body,
        mesh=mesh,
        in_specs=(
            P("tm", "tok", None),
            P(),
            P(),
            P(None, "tok"),
            P(None, "tok"),
            P(None, "tok"),
            P("tok", None),
        ),
        out_specs=P("tm", "tok", None),
        check_vma=False,
    )
```

profile of v0, /device:TPU:1, one launch (start us, length us, event | category | flops | bytes accessed | tf_op | source)
XLA Modules:
  0.0 548.5 jit_solution(11962400330113357791)
XLA Ops:
  6.5 0.0 all-gather.3.cloned.1.call-start
  6.5 1.9 pad_maximum_fusion
  8.5 0.0 all-gather.3.cloned.1.call-update
  8.5 0.0 all-reduce.2.cloned.1.call-start
  8.5 1.0 convert_reduce_fusion
  9.6 1.1 fusion.24
  10.7 113.7 %all-gather.3.cloned.1.call-done = bf16[3,1280,1024]{1,2,0:T(8,128)(2,1)} async-done(((bf16[3,1280,64]{1,2,0:T(8,128)(2,1)}), bf16[3,1280,1024]{1,2,0:T(8,128)(2,1)}) %all-gather.3.cloned.1.call-update) | async-done | bytes 7864336 | tf_op jit(solution)/shard_map/all_gather | solution.py:64
  124.5 5.8 %fusion.21 = bf16[3,1,64,1024]{3,2,0,1:T(8,128)(2,1)S(1)} fusion(bf16[3,1280,1024]{1,2,0:T(8,128)(2,1)} %all-gather.3.cloned.1.call-done, bf16[1,64,1280]{2,1,0:T(8,128)(2,1)} %param.9, f32[1280]{0:T(1024)} %param.11, f32[1280]{0:T(1024)} %param.10, f32[64]{0:T(128)S(1)} %add_rsqrt_fusion, f32[64]{0:T(128)S(1)} %broadcast_multiply_fusion), kind=kOutput, calls=%fused_computation.30 | convolution fusion | flops 504004608 | bytes 8432128 | tf_op jit(solution)/shard_map/td,nde->nte/dot_general | solution.py:61
  130.3 0.7 copy.20
  131.0 0.7 reshape.145
  131.7 16.1 %all_to_all.30 = bf16[16,2,6144]{2,1,0:T(2,128)(2,1)S(1)} all-to-all(bf16[16,2,6144]{2,1,0:T(2,128)(2,1)S(1)} %reshape.145), channel_id=1, replica_groups=mesh['tm'=32,'tok'=16] {'tok'}, dimensions={0} | all-to-all | bytes 786432 | tf_op jit(solution)/shard_map/all_to_all | solution.py:68
  147.9 0.6 reshape.146
  148.5 0.6 copy.30
  149.2 0.3 squeeze.17
  149.5 3.3 collective-permute-start
  152.8 4.4 collective-permute-done
  157.2 0.8 broadcast_select_fusion
  158.0 0.0 all-reduce.2.cloned.1.call-update
  158.0 0.0 all-gather.5.cloned.1.call-start
  158.1 0.7 all-gather.5.cloned.1.call-update
  158.8 0.2 reshape.138
  159.0 288.1 %all-reduce.2.cloned.1.call-done = bf16[2,1024,64]{1,2,0:T(8,128)(2,1)} async-done(((bf16[2,1024,64]{1,2,0:T(8,128)(2,1)}), bf16[2,1024,64]{1,2,0:T(8,128)(2,1)}) %all-reduce.2.cloned.1.call-update) | async-done | bytes 262160 | tf_op jit(solution)/shard_map/psum | solution.py:11
  447.2 1.0 slice_bitcast_fusion.1
  448.2 6.6 %while.17 = (s32[]{:T(128)}, bf16[2,512,1,64]{1,3,2,0:T(8,128)(2,1)S(1)}, bf16[2,512,1,64]{1,3,2,0:T(8,128)(2,1)S(1)}, bf16[1024,1,64]{0,2,1:T(8,128)(2,1)S(1)},...) while((s32[]{:T(128)}, ...), condition=%wide.region_8.9_spmd, body=%wide.region_3.8_spmd.sunk | while | flops 277937152 | bytes 13596769 | solution.py:95
  448.2 0.5 multiply_reduce_fusion.4
  448.7 0.5 multiply_reduce_fusion.5
  449.3 0.8 fusion.44
  450.1 0.7 fusion.45
  450.8 0.7 fusion.46
  451.5 0.5 multiply_reduce_fusion.4
  452.0 0.5 multiply_reduce_fusion.5
  452.6 0.8 fusion.44
  453.4 0.7 fusion.45
  454.1 0.7 fusion.46
  454.8 0.2 copy.27
  455.0 0.1 reshape.144
  455.1 0.5 broadcast.53
  455.6 2.3 reduce.10
  457.9 0.2 reshape.147
  458.2 38.8 %all_to_all.31 = bf16[16,2,2048]{2,1,0:T(2,128)(2,1)S(1)} all-to-all(bf16[16,2,2048]{2,1,0:T(2,128)(2,1)S(1)} %reshape.147), channel_id=1, replica_groups=mesh['tm'=32,'tok'=16] {'tok'}, dimensions={0} | all-to-all | bytes 262144 | tf_op jit(solution)/shard_map/all_to_all | solution.py:98
  497.0 0.3 reshape.148
  497.3 0.3 copy.25
  497.6 0.2 all_to_all.26
  497.8 0.4 copy.26
  498.2 0.2 reshape.141
  498.4 40.5 %all-gather.5.cloned.1.call-done = bf16[1024,1280]{1,0:T(8,128)(2,1)} async-done(((bf16[64,1280]{1,0:T(8,128)(2,1)}), bf16[1024,1280]{1,0:T(8,128)(2,1)}) %all-gather.5.cloned.1.call-update) | async-done | bytes 2621456 | tf_op jit(solution)/shard_map/all_gather | solution.py:102
  539.0 3.0 fusion.20
  (11 shorter events, 0.1 us)
Async XLA Ops:
  6.5 117.9 %all-gather.3.cloned.1.call-start = ((), (), s32[]{:S(2)}) async-start(), calls=%async_computation.2 | async-start | bytes 8355840 | tf_op jit(solution)/shard_map/all_gather | solution.py:64
  8.5 438.7 %all-reduce.2.cloned.1.call-start = ((), (), s32[]{:S(2)}) async-start(), calls=%async_computation.3 | async-start | bytes 524288 | tf_op jit(solution)/shard_map/psum | solution.py:11
  149.5 7.7 %collective-permute-start = (bf16[2,1024,64]{1,2,0:T(8,128)(2,1)S(1)}, bf16[2,1024,64]{1,2,0:T(8,128)(2,1)S(1)}, u32[]{:S(2)}, u32[]{:S(2)}) collective-permute-start(bf16[2,1024,64]{1,2,0:T(8,128)(2,1)S(1)} %squeeze.17), channel_id=1, source_target_pairs={{0,16},{16,32},{32,48},{48,64},{64,80},{80,96},{96,112},{112,128},... | collective-permute-start | bytes 786440 | tf_op jit(solution)/shard_map/ppermute | solution.py:17
  158.0 380.9 %all-gather.5.cloned.1.call-start = ((), (), s32[]{:S(2)}) async-start(), calls=%async_computation.4 | async-start | bytes 2785280 | tf_op jit(solution)/shard_map/all_gather | solution.py:102
Sparse Core Ops, SparseCore 0:
  10.7 113.7 all-gather.2
  158.1 288.9 all-reduce.1
  451.0 87.9 all-gather.4
where the time goes:
time: 549 us; the launch traced here: 548 us
  waiting for transfers between devices  448 us (82%)
  blocking collectives  55 us (10%)
  matrix products  13.7 us (2%)
  between operations  13.3 us (2%)
  other arithmetic  8.81 us (2%)
  local copies, waits for them, and re-layouts  6.78 us (1%)
    psum x1, waiting for transfers between devices, broadcast(): return lax.psum(kept, axis)  288 us
    all_gather x1, waiting for transfers between devices, body(): lax.all_gather(stacked, 'tok', axis=2, tiled=True)  114 us
    all_gather x1, waiting for transfers between devices, body(): lax.all_gather(out_weight, 'tok', axis=0, tiled=True)  40.5 us
    all_to_all x1, blocking collectives, body(): lax.all_to_all(attended, 'tok', split_axis=1, concat_axis=2, tiled=True)  38.8 us
    all_to_all x1, blocking collectives, body(): lax.all_to_all(projected, 'tok', split_axis=3, concat_axis=2, tiled=True)  16.1 us
  transfers between devices with their start and end apart: 4, of which 4 were waited for; matrix products, arithmetic and copies ran while one was open for 3% of the time, Pallas kernels for 0%

commit v1 on v0

v1 whole, which is shorter than its diff:
```python
import functools
import math

import jax
import jax.numpy as jnp
from jax import lax
from jax.experimental import pallas as pl
from jax.experimental.pallas import tpu as pltpu
from jax.sharding import PartitionSpec as P

MESH = pl.DeviceIdType.MESH
D = 1280
DH = 64
ROWS = 64
HALF = 32
TM = 32
TOK = 16
F32 = jnp.float32
BF16 = jnp.bfloat16
EXP_SCALE = DH ** (-0.5) / math.log(2.0)


def layer_norm(states, gain, bias):
    widened = states.astype(F32)
    center = jnp.mean(widened, axis=-1, keepdims=True)
    moved = widened - center
    spread = jnp.mean(jnp.square(moved), axis=-1, keepdims=True)
    return moved * lax.rsqrt(spread + 1e-05) * gain + bias


def kernel(
    x_hbm, gain_hbm, bias_hbm, wq_hbm, wk_hbm, wv_hbm, wo_hbm, o_ref,
    x_in, gain, bias, wq, wk, wv,
    wall, xg, wg, xf, apf, ap, apg, apgf, x0, akv, kv, pkv, qb, msend, mg, lhs,
    in_sem, tok_recv, tok_send, w_recv, w_send,
    sc_send, sc_recv, ap_send, ap_recv, an_send, an_recv,
    kv_send, kv_recv, mix_send, mix_recv, loc_sem,
):
    tm = lax.axis_index("tm")
    me = lax.axis_index("tok")
    y, x, c = me // 8, (me // 2) % 4, me % 2
    xp, xm, xa = (x + 1) % 4, (x + 3) % 4, (x + 2) % 4
    yo, co = 1 - y, 1 - c

    def tid(yy, xx, cc):
        return yy * 8 + xx * 2 + cc

    loads = []
    for i, (src, dst) in enumerate((
        (x_hbm.at[0], x_in), (gain_hbm, gain), (bias_hbm, bias), (wq_hbm, wq), (wk_hbm, wk), (wv_hbm, wv),
        (wo_hbm, wg.at[me]),
    )):
        load = pltpu.make_async_copy(src, dst, in_sem.at[i])
        load.start()
        loads.append(load)

    barrier = pltpu.get_barrier_semaphore()

    def greet_tok(i, carry):
        pl.semaphore_signal(barrier, inc=1, device_id=(tm, (me + i) % TOK), device_id_type=MESH)
        return carry

    def greet_tm(i, carry):
        pl.semaphore_signal(barrier, inc=1, device_id=((tm + i) % TM, me), device_id_type=MESH)
        return carry

    lax.fori_loop(1, TOK, greet_tok, 0)
    lax.fori_loop(1, TM, greet_tm, 0)

    for load in loads[:3]:
        load.wait()
    normed = layer_norm(x_in[...], gain[...], bias[...])
    xg[me] = normed.astype(BF16)

    @pl.when(tm == 0)
    def _():
        apf[...] = jnp.zeros_like(apf)
        xf[...] = normed
        for k in range(20):
            apf[pl.ds(k, TM, stride=32), :] = xf[(k % 2) * 32 : (k % 2) * 32 + 32, (k // 2) * 128 : (k // 2) * 128 + 128]
        ap[...] = apf[...].reshape(TM, 32, 128).astype(BF16)

    for load in loads[3:]:
        load.wait()
    wall[:, 0:128] = jnp.concatenate([wk[...], wv[...]], axis=1)
    wall[:, 128:256] = jnp.concatenate([wq[...], jnp.zeros_like(wq)], axis=1)

    pl.semaphore_wait(barrier, TOK - 1 + TM - 1)

    def scatter(j):
        return pltpu.make_async_remote_copy(
            src_ref=ap.at[j], dst_ref=apg.at[me], send_sem=sc_send.at[j], recv_sem=sc_recv,
            device_id=(j, me), device_id_type=MESH)

    @pl.when(tm == 0)
    def _():
        def go(j, carry):
            scatter(j).start()
            return carry
        lax.fori_loop(1, TM, go, 0)

    pending = []

    class Gather:
        def __init__(self, buf, send, recv):
            self.buf, self.send_sem, self.recv, self.count = buf, send, recv, 0

        def part(self, block, half):
            return self.buf.at[block, pl.ds(half * HALF, HALF)]

        def send(self, block, half, to):
            copy = pltpu.make_async_remote_copy(
                src_ref=self.part(block, half), dst_ref=self.part(block, half),
                send_sem=self.send_sem.at[self.count], recv_sem=self.recv.at[block * 2 + half],
                device_id=(tm, to), device_id_type=MESH)
            self.count += 1
            copy.start()
            pending.append(copy)

        def wait(self, block, half):
            part = self.part(block, half)
            pltpu.make_async_copy(part, part, self.recv.at[block * 2 + half]).wait()

        def wait_block(self, block):
            self.wait(block, 0)
            self.wait(block, 1)

    right, left, over, twin = tid(y, xp, c), tid(y, xm, c), tid(yo, x, c), tid(y, x, co)
    tok = Gather(xg, tok_send, tok_recv)
    out = Gather(wg, w_send, w_recv)

    def own_y(g):
        g.send(me, 0, over)
        g.send(me, 1, over)

    def own_x(g):
        for half in (0, 1):
            g.send(me, half, right)
            g.send(me, half, left)
            g.send(me, half, twin)

    def relay(g, yy):
        from_left, from_right = tid(yy, xm, c), tid(yy, xp, c)
        g.wait(from_left, 0)
        g.send(from_left, 0, right)
        g.wait(from_right, 1)
        g.send(from_right, 1, left)
        g.send(from_left, 0, twin)
        g.send(from_right, 1, twin)
        g.wait(from_left, 1)
        g.send(from_left, 1, twin)
        g.wait(from_right, 0)
        g.send(from_right, 0, twin)

    def spread_over(g):
        for half in (0, 1):
            g.wait(over, half)
            g.send(over, half, right)
            g.send(over, half, left)
            g.send(over, half, twin)

    def far(g, yy):
        block = tid(yy, xa, c)
        for half in (0, 1):
            g.wait(block, half)
            g.send(block, half, twin)

    def kv_copy(chip):
        rows = pl.ds(chip * 128, 128)
        return pltpu.make_async_remote_copy(
            src_ref=kv.at[rows], dst_ref=pkv.at[rows], send_sem=kv_send.at[chip], recv_sem=kv_recv.at[chip],
            device_id=(jnp.minimum(tm + 1, TM - 1), me), device_id_type=MESH)

    def project(yy, xx):
        chip = yy * 4 + xx
        tokens = xg[pl.ds(chip * 2, 2)].reshape(128, D)
        made = jnp.dot(tokens, wall[...], preferred_element_type=F32).astype(BF16)
        rows = pl.ds(chip * 128, 128)
        kv[rows] = made[:, 0:128]
        qb[rows] = made[:, 128:256]

        @pl.when(tm < TM - 1)
        def _():
            kv_copy(chip).start()

    own_y(tok)
    own_x(tok)
    tok.wait_block(twin)
    project(y, x)
    relay(tok, y)

    @pl.when(tm > 0)
    def _():
        pltpu.make_async_copy(apg.at[me], apg.at[me], sc_recv).wait()

    @pl.when(tm == 0)
    def _():
        apg[me] = ap[0]

    def piece(i):
        to = (me + i) % TOK
        return pltpu.make_async_remote_copy(
            src_ref=apg.at[me], dst_ref=apg.at[me], send_sem=ap_send.at[i], recv_sem=ap_recv.at[me],
            device_id=(tm, to), device_id_type=MESH)

    def send_piece(i, carry):
        piece(i).start()
        return carry

    lax.fori_loop(1, TOK, send_piece, 0)

    for xx in (xm, xp):
        tok.wait_block(tid(y, xx, co))
        project(y, xx)
    spread_over(tok)
    far(tok, y)

    def wait_piece(i, carry):
        s = (me + i) % TOK
        pltpu.make_async_copy(apg.at[s], apg.at[s], ap_recv.at[s]).wait()
        return carry

    lax.fori_loop(1, TOK, wait_piece, 0)
    apgf[...] = apg[...].astype(F32).reshape(TOK * 32, 128)
    for k in range(20):
        x0[(k % 2) * 16 : (k % 2) * 16 + 16, (k // 2) * 128 : (k // 2) * 128 + 128] = (
            apgf[pl.ds(k, TOK, stride=32), :].astype(BF16))
    akv[pl.ds(tm * 32, 32)] = jnp.dot(x0[...], wall[:, 0:128], preferred_element_type=F32).astype(BF16)

    def anchor(i):
        rows = pl.ds(tm * 32, 32)
        return pltpu.make_async_remote_copy(
            src_ref=akv.at[rows], dst_ref=akv.at[rows], send_sem=an_send.at[i], recv_sem=an_recv.at[tm],
            device_id=((tm + i) % TM, me), device_id_type=MESH)

    def send_anchor(i, carry):
        anchor(i).start()
        return carry

    lax.fori_loop(1, TM, send_anchor, 0)

    tok.wait_block(tid(y, xa, co))
    project(y, xa)
    own_y(out)
    tok.wait_block(tid(yo, x, co))
    project(yo, x)
    relay(tok, yo)
    for xx in (xm, xp):
        tok.wait_block(tid(yo, xx, co))
        project(yo, xx)
    far(tok, yo)
    own_x(out)
    tok.wait_block(tid(yo, xa, co))
    project(yo, xa)

    def wait_anchor(i, carry):
        rows = pl.ds(((tm + i) % TM) * 32, 32)
        pltpu.make_async_copy(akv.at[rows], akv.at[rows], an_recv.at[(tm + i) % TM]).wait()
        return carry

    lax.fori_loop(1, TM, wait_anchor, 0)

    @pl.when(tm == 0)
    def _():
        copy = pltpu.make_async_copy(kv, pkv, loc_sem)
        copy.start()
        copy.wait()

    @pl.when(tm > 0)
    def _():
        for chip in range(8):
            rows = pl.ds(chip * 128, 128)
            pltpu.make_async_copy(pkv.at[rows], pkv.at[rows], kv_recv.at[chip]).wait()

    low = lax.broadcasted_iota(jnp.int32, (HALF, 128), 1) < DH
    nt = (((1,), (1,)), ((), ()))

    def mix_copy(to):
        return pltpu.make_async_remote_copy(
            src_ref=msend.at[to], dst_ref=mg.at[me], send_sem=mix_send.at[to], recv_sem=mix_recv.at[me],
            device_id=(tm, to), device_id_type=MESH)

    def attend(i):
        yy = (y + 1 + i // 2) % 2
        pp = (x // 2 + 1 + i) % 2
        first = yy * 8 + pp * 4
        queries = qb[pl.ds(first * ROWS, 4 * ROWS)]
        s_a = lax.dot_general(queries, akv[...], nt, preferred_element_type=F32)
        s_p = lax.dot_general(queries, pkv[...], nt, preferred_element_type=F32)
        highest = jnp.maximum(jnp.max(s_a, axis=-1, keepdims=True), jnp.max(s_p, axis=-1, keepdims=True))
        e_a = jnp.exp2((s_a - highest) * EXP_SCALE)
        e_p = jnp.exp2((s_p - highest) * EXP_SCALE)
        inverse = 1.0 / (jnp.sum(e_a, axis=-1, keepdims=True) + jnp.sum(e_p, axis=-1, keepdims=True))
        p_a = (e_a * inverse).astype(BF16)
        p_p = (e_p * inverse).astype(BF16)
        mixed = jnp.dot(p_a, akv[...], preferred_element_type=F32) + jnp.dot(p_p, pkv[...], preferred_element_type=F32)
        for k in range(4):
            top = mixed[k * ROWS : k * ROWS + HALF]
            bottom = mixed[k * ROWS + HALF : (k + 1) * ROWS]
            msend[first + k] = jnp.where(low, pltpu.roll(top, DH, 1), bottom).astype(BF16)
            to = first + k

            @pl.when(to != me)
            def _():
                mix_copy(to).start()

    def two(start):
        lax.fori_loop(start, start + 2, lambda i, carry: (attend(i), carry)[1], 0)

    two(0)
    relay(out, y)
    spread_over(out)
    two(2)
    far(out, y)
    relay(out, yo)
    far(out, yo)
    mg[me] = msend[me]

    def wait_mix(i, carry):
        s = (me + i) % TOK
        pltpu.make_async_copy(mg.at[s], mg.at[s], mix_recv.at[s]).wait()
        return carry

    lax.fori_loop(1, TOK, wait_mix, 0)
    for i in range(8):
        even = mg[2 * i].astype(F32)
        odd = mg[2 * i + 1].astype(F32)
        lhs[0:HALF, i * 128 : (i + 1) * 128] = jnp.where(low, even, pltpu.roll(odd, DH, 1)).astype(BF16)
        lhs[HALF:ROWS, i * 128 : (i + 1) * 128] = jnp.where(low, pltpu.roll(even, DH, 1), odd).astype(BF16)
    for yy in (0, 1):
        for xx in range(4):
            @pl.when((yy != y) | (xx != x))
            def _():
                out.wait_block(tid(yy, xx, co))
    out.wait_block(twin)
    o_ref[0] = jnp.dot(lhs[...], wg[...].reshape(TOK * DH, D), preferred_element_type=F32).astype(BF16)

    for copy in pending:
        copy.wait_send()

    def drain_tok(i, carry):
        piece(i).wait_send()
        mix_copy((me + i) % TOK).wait_send()
        return carry

    def drain_tm(i, carry):
        anchor(i).wait_send()
        return carry

    lax.fori_loop(1, TOK, drain_tok, 0)
    lax.fori_loop(1, TM, drain_tm, 0)

    @pl.when(tm == 0)
    def _():
        def drain(j, carry):
            scatter(j).wait_send()
            return carry
        lax.fori_loop(1, TM, drain, 0)

    @pl.when(tm < TM - 1)
    def _():
        for chip in range(8):
            kv_copy(chip).wait_send()


def body(hidden_states, norm_gain, norm_bias, q_weight, k_weight, v_weight, out_weight):
    anywhere = pl.BlockSpec(memory_space=pl.ANY)
    vmem = pltpu.VMEM
    dma = pltpu.SemaphoreType.DMA
    return pl.pallas_call(
        kernel,
        out_shape=jax.ShapeDtypeStruct((1, ROWS, D), BF16),
        in_specs=[anywhere] * 7,
        out_specs=pl.BlockSpec(memory_space=pltpu.VMEM),
        scratch_shapes=[
            vmem((ROWS, D), BF16), vmem((1, D), F32), vmem((1, D), F32),
            vmem((D, DH), BF16), vmem((D, DH), BF16), vmem((D, DH), BF16),
            vmem((D, 256), BF16),
            vmem((TOK, ROWS, D), BF16),
            vmem((TOK, ROWS, D), BF16),
            vmem((ROWS, D), F32),
            vmem((TM * 32, 128), F32),
            vmem((TM, 32, 128), BF16),
            vmem((TOK, 32, 128), BF16),
            vmem((TOK * 32, 128), F32),
            vmem((32, D), BF16),
            vmem((1024, 128), BF16),
            vmem((1024, 128), BF16),
            vmem((1024, 128), BF16),
            vmem((1024, 128), BF16),
            vmem((TOK, HALF, 128), BF16),
            vmem((TOK, HALF, 128), BF16),
            vmem((ROWS, TOK * DH), BF16),
            dma((7,)), dma((32,)), dma((40,)), dma((32,)), dma((40,)),
            dma((TM,)), dma, dma((TOK,)), dma((TOK,)), dma((TM,)), dma((TM,)),
            dma((8,)), dma((8,)), dma((TOK,)), dma((TOK,)), dma,
        ],
        compiler_params=pltpu.CompilerParams(
            collective_id=0, has_side_effects=True, vmem_limit_bytes=40 * 2**20),
        cost_estimate=pl.CostEstimate(flops=1_200_000_000, bytes_accessed=2_000_000, transcendentals=2_000_000),
        name="cross_frame_attention",
    )(hidden_states, norm_gain.reshape(1, D), norm_bias.reshape(1, D), q_weight, k_weight, v_weight, out_weight)


def solution(mesh):
    return jax.shard_map(
        body,
        mesh=mesh,
        in_specs=(P("tm", "tok", None), P(), P(), P(None, "tok"), P(None, "tok"), P(None, "tok"), P("tok", None)),
        out_specs=P("tm", "tok", None),
        check_vma=False,
    )
```

time: 549 us -> 73.4 us (0.13)
  the two profiles are of different devices: /device:TPU:1 before, /device:TPU:19 now
where the time goes in v1:
time: 73.4 us; the launch traced here: 73.2 us
  Pallas kernels  68.7 us (94%)
  local copies, waits for them, and re-layouts  4.47 us (6%)
    pallas_call x1, Pallas kernels, body(): pl.pallas_call(kernel, out_shape=jax.ShapeDtypeStruct((1, ROWS, D), BF16)...  68.7 us
    unnamed x14, local copies, waits for them, and re-layouts  3.75 us

profile of v1, /device:TPU:19, one launch (start us, length us, event | category | flops | bytes accessed | tf_op | source)
XLA Modules:
  0.0 73.2 jit_solution(13035669747231180967)
XLA Ops:
  0.0 0.0 copy-start.4
  0.0 0.7 reshape.6.gain_hbm
  0.7 0.0 copy-done.4
  0.7 0.0 copy-start.2
  0.7 1.2 %copy.8.wq_hbm = bf16[1280,64]{1,0:T(8,128)(2,1)S(1)} copy(bf16[1280,64]{0,1:T(8,128)(2,1)} %param.10) | data formatting | bytes 327680 | tf_op args[3]
  1.9 0.0 copy-done.2
  1.9 0.0 copy-start.3
  1.9 0.2 copy.9.wk_hbm
  2.2 0.7 copy-done.3
  2.8 0.0 copy-start
  2.8 0.0 copy-start.1
  2.8 0.2 copy.10.wv_hbm
  3.1 0.7 copy-done
  3.8 0.1 copy-done.1
  3.8 68.7 %cross_frame_attention.1 = bf16[1,64,1280]{2,1,0:T(8,128)(2,1)S(1)} custom-call(bf16[1,64,1280]{2,1,0:T(8,128)(2,1)S(1)} %copy-done, f32[1,1280]{1,0:T(1,128)S(1)} %reshape.6.gain_hbm, f32[1,1280]{1,0:T(1,128)S(1)} %reshape.7.bias_hbm, bf16[1280,64]{1,0:T(8,128)(2,1)S(1)} %copy.8.wq_hbm, bf16[1280,64]{1,0:T(8,128)(2,1)S(1)} %copy.9.wk_hbm, ...), custom_call_target="tpu_custom_call" | custom-call | flops 1200000000 | bytes 2000000 | tf_op jit(solution)/shard_map/cross_frame_attention/pallas_call | solution.py:370
  72.5 0.7 copy.12
  (1 shorter events, 0.0 us)
Async XLA Ops:
  0.0 0.7 copy-start.4
  0.7 1.2 %copy-start.2 = (bf16[1280,64]{0,1:T(8,128)(2,1)S(1)}, bf16[1280,64]{0,1:T(8,128)(2,1)}, u32[]{:S(2)}) copy-start(bf16[1280,64]{0,1:T(8,128)(2,1)} %param.11) | copy-start | bytes 491524
  1.9 0.9 %copy-start.3 = (bf16[1280,64]{0,1:T(8,128)(2,1)S(1)}, bf16[1280,64]{0,1:T(8,128)(2,1)}, u32[]{:S(2)}) copy-start(bf16[1280,64]{0,1:T(8,128)(2,1)} %param.12) | copy-start | bytes 491524
  2.8 0.9 %copy-start = (bf16[1,64,1280]{2,1,0:T(8,128)(2,1)S(1)}, bf16[1,64,1280]{2,1,0:T(8,128)(2,1)}, u32[]{:S(2)}) copy-start(bf16[1,64,1280]{2,1,0:T(8,128)(2,1)} %x_hbm.1) | copy-start | bytes 491524
  2.8 1.0 %copy-start.1 = (bf16[64,1280]{1,0:T(8,128)(2,1)S(1)}, bf16[64,1280]{1,0:T(8,128)(2,1)}, u32[]{:S(2)}) copy-start(bf16[64,1280]{1,0:T(8,128)(2,1)} %wo_hbm.1) | copy-start | bytes 491524

commit v2 on v1

v2 whole, which is shorter than its diff:
```python
import functools
import math

import jax
import jax.numpy as jnp
from jax import lax
from jax.experimental import pallas as pl
from jax.experimental.pallas import tpu as pltpu
from jax.sharding import PartitionSpec as P

MESH = pl.DeviceIdType.MESH
D = 1280
DH = 64
ROWS = 64
HALF = 32
TM = 32
TOK = 16
F32 = jnp.float32
BF16 = jnp.bfloat16
EXP_SCALE = DH ** (-0.5) / math.log(2.0)


def layer_norm(states, gain, bias):
    widened = states.astype(F32)
    center = jnp.mean(widened, axis=-1, keepdims=True)
    moved = widened - center
    spread = jnp.mean(jnp.square(moved), axis=-1, keepdims=True)
    return moved * lax.rsqrt(spread + 1e-05) * gain + bias


def kernel(
    x_hbm, gain_hbm, bias_hbm, wq_hbm, wk_hbm, wv_hbm, wo_hbm, o_ref,
    x_in, gain, bias, wall_t,
    wall, xg, wg, xf, apf, ap, apz, apg, apgf, x0, akv, kv, pkv, qb, e_prev, m_prev, l_prev, msend, mg, lhs,
    in_sem, tok_recv, tok_send, w_recv, w_send,
    sc_send, sc_recv, sy_send, sy_recv, ap_send, ap_recv, an_send, an_recv,
    kv_send, kv_recv, mix_send, mix_recv, loc_sem,
):
    tm = lax.axis_index("tm")
    y_lo, z = tm // 8, tm % 8
    me = lax.axis_index("tok")
    y, x, c = me // 8, (me // 2) % 4, me % 2
    xp, xm, xa = (x + 1) % 4, (x + 3) % 4, (x + 2) % 4
    yo, co = 1 - y, 1 - c

    def tid(yy, xx, cc):
        return yy * 8 + xx * 2 + cc

    loads = []
    for i, (src, dst) in enumerate((
        (x_hbm.at[0], x_in), (gain_hbm, gain), (bias_hbm, bias),
        (wk_hbm, wall_t.at[pl.ds(0, DH)]), (wv_hbm, wall_t.at[pl.ds(DH, DH)]), (wq_hbm, wall_t.at[pl.ds(2 * DH, DH)]),
        (wo_hbm, wg.at[me]),
    )):
        load = pltpu.make_async_copy(src, dst, in_sem.at[i])
        load.start()
        loads.append(load)

    barrier = pltpu.get_barrier_semaphore()

    def greet_tok(i, carry):
        pl.semaphore_signal(barrier, inc=1, device_id=(tm, (me + i) % TOK), device_id_type=MESH)
        return carry

    def greet_z(i, carry):
        pl.semaphore_signal(barrier, inc=1, device_id=(y_lo * 8 + (z + i) % 8, me), device_id_type=MESH)
        return carry

    def greet_y(i, carry):
        pl.semaphore_signal(barrier, inc=1, device_id=((tm + 8 * i) % TM, me), device_id_type=MESH)
        return carry

    lax.fori_loop(1, 4, greet_y, 0)
    lax.fori_loop(1, 8, greet_z, 0)
    for step in (1, TM - 1):
        pl.semaphore_signal(barrier, inc=1, device_id=((tm + step) % TM, me), device_id_type=MESH)
    lax.fori_loop(1, TOK, greet_tok, 0)

    for load in loads[:3]:
        load.wait()
    normed = layer_norm(x_in[...], gain[...].reshape(1, D), bias[...].reshape(1, D))
    xg[me] = normed.astype(BF16)

    @pl.when(tm == 0)
    def _():
        apf[...] = jnp.zeros_like(apf)
        xf[...] = normed
        for k in range(20):
            apf[pl.ds(k, TM, stride=32), :] = xf[(k % 2) * 32 : (k % 2) * 32 + 32, (k // 2) * 128 : (k // 2) * 128 + 128]
        ap[...] = apf[...].reshape(8, 4, 32, 128).astype(BF16)

    wall_t[3 * DH :] = jnp.zeros((DH, D), BF16)
    for load in loads[3:]:
        load.wait()
    wall[...] = wall_t[...].T

    pl.semaphore_wait(barrier, TOK - 1 + 7 + 3 + 2)

    def scatter(j):
        return pltpu.make_async_remote_copy(
            src_ref=ap.at[j], dst_ref=apz, send_sem=sc_send.at[j], recv_sem=sc_recv,
            device_id=(j, me), device_id_type=MESH)

    def scatter_y(k):
        return pltpu.make_async_remote_copy(
            src_ref=apz.at[k], dst_ref=apg.at[me], send_sem=sy_send.at[k], recv_sem=sy_recv,
            device_id=(k * 8 + z, me), device_id_type=MESH)

    @pl.when(tm == 0)
    def _():
        for j in (4, 3, 5, 2, 6, 1, 7):
            scatter(j).start()
        apz[...] = ap[0]

    class Gather:
        def __init__(self, buf, send, recv):
            self.buf, self.send_sem, self.recv, self.count, self.sent = buf, send, recv, 0, []

        def part(self, block, piece):
            return self.buf.at[block, pl.ds(piece[0], piece[1])]

        def send(self, block, piece, to, group=None):
            copy = pltpu.make_async_remote_copy(
                src_ref=self.part(block, piece), dst_ref=self.part(block, piece),
                send_sem=self.send_sem.at[self.count], recv_sem=self.recv.at[block * 4 + piece[0] // 16],
                device_id=(tm if group is None else group, to), device_id_type=MESH)
            self.count += 1
            copy.start()
            self.sent.append(copy)

        def wait(self, block, piece):
            part = self.part(block, piece)
            pltpu.make_async_copy(part, part, self.recv.at[block * 4 + piece[0] // 16]).wait()

        def wait_block(self, block, pieces):
            for piece in pieces:
                self.wait(block, piece)

    halves = ((0, 32), (32, 32))
    quarters = ((0, 16), (16, 16), (32, 16), (48, 16))
    right, left, over, twin = tid(y, xp, c), tid(y, xm, c), tid(yo, x, c), tid(y, x, co)
    tok = Gather(xg, tok_send, tok_recv)
    out = Gather(wg, w_send, w_recv)

    def own_x(g):
        for piece in halves:
            g.send(me, piece, right)
            g.send(me, piece, left)
        for piece in halves:
            g.send(me, piece, twin)

    def relay_even(g, yy, even):
        from_left, from_right = tid(yy, xm, c), tid(yy, xp, c)
        g.wait(from_left, even)
        g.send(from_left, even, right)
        g.wait(from_right, even)
        g.send(from_left, even, twin)
        g.send(from_right, even, twin)

    def relay_odd(g, yy, odd):
        from_left, from_right = tid(yy, xm, c), tid(yy, xp, c)
        g.wait(from_right, odd)
        g.send(from_right, odd, left)
        g.wait(from_left, odd)
        g.send(from_left, odd, twin)
        g.send(from_right, odd, twin)

    def relay(g, yy, pieces):
        for even, odd in zip(pieces[::2], pieces[1::2]):
            relay_even(g, yy, even)
            relay_odd(g, yy, odd)

    def spread_over(g, piece):
        g.send(over, piece, right)
        g.send(over, piece, left)
        g.send(over, piece, twin)

    def far(g, yy, pieces):
        block = tid(yy, xa, c)
        for piece in pieces:
            g.wait(block, piece)
            g.send(block, piece, twin)

    def kv_copy(chip):
        rows = pl.ds(chip * 128, 128)
        return pltpu.make_async_remote_copy(
            src_ref=kv.at[rows], dst_ref=pkv.at[rows], send_sem=kv_send.at[chip], recv_sem=kv_recv.at[chip],
            device_id=(jnp.minimum(tm + 1, TM - 1), me), device_id_type=MESH)

    def project(yy, xx):
        chip = yy * 4 + xx
        tokens = xg[pl.ds(chip * 2, 2)].reshape(128, D)
        made = jnp.dot(tokens, wall[...], preferred_element_type=F32).astype(BF16)
        rows = pl.ds(chip * 128, 128)
        kv[rows] = made[:, 0:128]
        qb[rows] = made[:, 128:256]

        @pl.when(tm < TM - 1)
        def _():
            kv_copy(chip).start()

    def rows_copy(i):
        return pltpu.make_async_remote_copy(
            src_ref=apg.at[me], dst_ref=apg.at[me], send_sem=ap_send.at[i], recv_sem=ap_recv.at[me],
            device_id=(tm, (me + i) % TOK), device_id_type=MESH)

    def wait_rows(slot):
        pltpu.make_async_copy(apg.at[slot], apg.at[slot], ap_recv.at[slot]).wait()

    def each(start, stop, step):
        lax.fori_loop(start, stop, lambda i, carry: (step(i), carry)[1], 0)

    def half_z(zz):
        return pl.ds(y_lo * 128 + zz * 16, 16)

    def half_zy(yy):
        return pl.ds(yy * 128, 128)

    def half_y(yy):
        return pl.ds(512 + z * 64 + yy * 16, 16)

    def half_yz(zz):
        return pl.ds(512 + zz * 64, 64)

    def anchor(rows, n, source, to):
        return pltpu.make_async_remote_copy(
            src_ref=akv.at[rows], dst_ref=akv.at[rows], send_sem=an_send.at[n], recv_sem=an_recv.at[source],
            device_id=(to, me), device_id_type=MESH)

    def wait_anchor(rows, source):
        pltpu.make_async_copy(akv.at[rows], akv.at[rows], an_recv.at[source]).wait()

    def anchor_z(i):
        return anchor(half_z(z), i, z, y_lo * 8 + (z + i) % 8)

    def anchor_y(i):
        return anchor(half_y(y_lo), 8 + i, 8 + y_lo, (tm + 8 * i) % TM)

    def anchor_zy(i):
        return anchor(half_zy(y_lo), 12 + i, 12 + y_lo, (tm + 8 * i) % TM)

    def anchor_yz(i):
        return anchor(half_yz(z), 16 + i, 16 + z, y_lo * 8 + (z + i) % 8)

    def over_in(piece):
        tok.wait(over, piece)
        spread_over(tok, piece)

    tok.send(me, quarters[0], over)
    tok.send(me, halves[0], right)
    tok.send(me, halves[0], left)
    tok.send(me, quarters[1], over)
    tok.send(me, halves[1], right)
    tok.send(me, halves[1], left)
    tok.send(me, quarters[2], over)
    tok.send(me, halves[0], twin)
    tok.send(me, halves[1], twin)
    tok.send(me, quarters[3], over)

    tok.wait_block(twin, halves)
    project(y, x)

    @pl.when(tm < 8)
    def _():
        @pl.when(tm > 0)
        def _():
            pltpu.make_async_copy(apz, apz, sc_recv).wait()
        for k in (3, 2, 1):
            scatter_y(k).start()
        apg[me] = apz[0]

    relay_even(tok, y, halves[0])
    over_in(quarters[0])
    relay_odd(tok, y, halves[1])
    over_in(quarters[1])

    for xx in (xm, xp):
        tok.wait_block(tid(y, xx, co), halves)
        project(y, xx)
    over_in(quarters[2])
    over_in(quarters[3])

    @pl.when(tm >= 8)
    def _():
        pltpu.make_async_copy(apg.at[me], apg.at[me], sy_recv).wait()

    each(1, TOK, lambda i: rows_copy(i).start())
    far(tok, y, halves)
    relay(tok, yo, quarters[:2])
    tok.wait_block(tid(y, xa, co), halves)
    project(y, xa)
    relay(tok, yo, quarters[2:])
    mine, theirs = (32 * (z % 2), 32), (32 - 32 * (z % 2), 32)
    out.send(me, mine, over)
    own_x(out)
    tok.wait_block(tid(yo, x, co), quarters)
    project(yo, x)
    for xx in (xm, xp):
        tok.wait_block(tid(yo, xx, co), quarters)
        project(yo, xx)

    each(1, TOK, lambda i: wait_rows((me + i) % TOK))
    apgf[...] = apg[...].astype(F32).reshape(TOK * 32, 128)
    for k in range(20):
        x0[(k % 2) * 16 : (k % 2) * 16 + 16, (k // 2) * 128 : (k // 2) * 128 + 128] = (
            apgf[pl.ds(k, TOK, stride=32), :].astype(BF16))
    made = jnp.dot(x0[...], wall[:, 0:128], preferred_element_type=F32).astype(BF16)
    akv[half_z(z)] = made[0:16]
    akv[half_y(y_lo)] = made[16:32]
    each(1, 4, lambda i: anchor_y(i).start())
    each(1, 8, lambda i: anchor_z(i).start())

    far(tok, yo, quarters)
    tok.wait_block(tid(yo, xa, co), quarters)
    project(yo, xa)
    out.wait(over, mine)
    out.send(over, mine, me, tm + 1 - 2 * (z % 2))
    each(1, 4, lambda i: wait_anchor(half_y((y_lo + i) % 4), 8 + (y_lo + i) % 4))
    each(1, 8, lambda i: anchor_yz(i).start())
    each(1, 8, lambda i: wait_anchor(half_z((z + i) % 8), (z + i) % 8))
    each(1, 4, lambda i: anchor_zy(i).start())

    @pl.when(tm == 0)
    def _():
        copy = pltpu.make_async_copy(kv, pkv, loc_sem)
        copy.start()
        copy.wait()

    @pl.when(tm > 0)
    def _():
        for chip in range(8):
            rows = pl.ds(chip * 128, 128)
            pltpu.make_async_copy(pkv.at[rows], pkv.at[rows], kv_recv.at[chip]).wait()

    low = lax.broadcasted_iota(jnp.int32, (HALF, 128), 1) < DH
    nt = (((1,), (1,)), ((), ()))

    def mix_copy(to):
        return pltpu.make_async_remote_copy(
            src_ref=msend.at[to], dst_ref=mg.at[me], send_sem=mix_send.at[to], recv_sem=mix_recv.at[me],
            device_id=(tm, to), device_id_type=MESH)

    def chunk(i):
        yy = (y + 1 + i // 2) % 2
        pp = (x // 2 + 1 + i) % 2
        return yy * 8 + pp * 4

    def attend_prev(i):
        rows = pl.ds(chunk(i) * ROWS, 4 * ROWS)
        scores = lax.dot_general(qb[rows], pkv[...], nt, preferred_element_type=F32)
        highest = jnp.max(scores, axis=-1, keepdims=True)
        weights = jnp.exp2((scores - highest) * EXP_SCALE)
        e_prev[rows] = weights
        m_prev[rows] = jnp.broadcast_to(highest, (4 * ROWS, 128))
        l_prev[rows] = jnp.broadcast_to(jnp.sum(weights, axis=-1, keepdims=True), (4 * ROWS, 128))

    def attend(i):
        first = chunk(i)
        rows = pl.ds(first * ROWS, 4 * ROWS)
        scores = lax.dot_general(qb[rows], akv[...], nt, preferred_element_type=F32)
        before = m_prev[rows][:, 0:1]
        highest = jnp.maximum(jnp.max(scores, axis=-1, keepdims=True), before)
        weights = jnp.exp2((scores - highest) * EXP_SCALE)
        shrink = jnp.exp2((before - highest) * EXP_SCALE)
        inverse = 1.0 / (jnp.sum(weights, axis=-1, keepdims=True) + l_prev[rows][:, 0:1] * shrink)
        p_a = (weights * inverse).astype(BF16)
        p_p = (e_prev[rows] * (shrink * inverse)).astype(BF16)
        mixed = jnp.dot(p_a, akv[...], preferred_element_type=F32) + jnp.dot(p_p, pkv[...], preferred_element_type=F32)
        for k in range(4):
            top = mixed[k * ROWS : k * ROWS + HALF]
            bottom = mixed[k * ROWS + HALF : (k + 1) * ROWS]
            msend[first + k] = jnp.where(low, pltpu.roll(top, DH, 1), bottom).astype(BF16)
            to = first + k

            @pl.when(to != me)
            def _():
                mix_copy(to).start()

    out.wait(over, theirs)
    for piece in halves:
        spread_over(out, piece)
    each(0, 4, attend_prev)
    relay(out, y, halves)
    each(1, 8, lambda i: wait_anchor(half_yz((z + i) % 8), 16 + (z + i) % 8))
    each(1, 4, lambda i: wait_anchor(half_zy((y_lo + i) % 4), 12 + (y_lo + i) % 4))
    each(0, 2, attend)
    relay(out, yo, halves)
    far(out, y, halves)
    each(2, 4, attend)
    far(out, yo, halves)
    mg[me] = msend[me]

    def drain_mix(i, carry):
        mix_copy((me + i) % TOK).wait_send()
        return carry

    each(1, TOK, lambda i: rows_copy(i).wait_send())
    each(1, 8, lambda i: anchor_z(i).wait_send())
    each(1, 4, lambda i: anchor_y(i).wait_send())
    each(1, 4, lambda i: anchor_zy(i).wait_send())
    each(1, 8, lambda i: anchor_yz(i).wait_send())

    @pl.when(tm == 0)
    def _():
        for j in range(1, 8):
            scatter(j).wait_send()

    @pl.when(tm < 8)
    def _():
        for k in range(1, 4):
            scatter_y(k).wait_send()

    @pl.when(tm < TM - 1)
    def _():
        for chip in range(8):
            kv_copy(chip).wait_send()

    for copy in tok.sent:
        copy.wait_send()

    def wait_mix(i, carry):
        s = (me + i) % TOK
        pltpu.make_async_copy(mg.at[s], mg.at[s], mix_recv.at[s]).wait()
        return carry

    lax.fori_loop(1, TOK, wait_mix, 0)
    for i in range(8):
        even = mg[2 * i].astype(F32)
        odd = mg[2 * i + 1].astype(F32)
        lhs[0:HALF, i * 128 : (i + 1) * 128] = jnp.where(low, even, pltpu.roll(odd, DH, 1)).astype(BF16)
        lhs[HALF:ROWS, i * 128 : (i + 1) * 128] = jnp.where(low, pltpu.roll(even, DH, 1), odd).astype(BF16)
    for yy in (0, 1):
        for xx in range(4):
            @pl.when((yy != y) | (xx != x))
            def _():
                out.wait_block(tid(yy, xx, co), halves)
    out.wait_block(twin, halves)
    o_ref[0] = jnp.dot(lhs[...], wg[...].reshape(TOK * DH, D), preferred_element_type=F32).astype(BF16)

    for copy in out.sent:
        copy.wait_send()
    lax.fori_loop(1, TOK, drain_mix, 0)


def body(hidden_states, norm_gain, norm_bias, q_weight, k_weight, v_weight, out_weight):
    anywhere = pl.BlockSpec(memory_space=pltpu.HBM)
    vmem = pltpu.VMEM
    dma = pltpu.SemaphoreType.DMA
    return pl.pallas_call(
        kernel,
        out_shape=jax.ShapeDtypeStruct((1, ROWS, D), BF16),
        in_specs=[anywhere] * 7,
        out_specs=pl.BlockSpec(memory_space=pltpu.VMEM),
        scratch_shapes=[
            vmem((ROWS, D), BF16), vmem((D,), F32), vmem((D,), F32),
            vmem((256, D), BF16),
            vmem((D, 256), BF16),
            vmem((TOK, ROWS, D), BF16),
            vmem((TOK, ROWS, D), BF16),
            vmem((ROWS, D), F32),
            vmem((TM * 32, 128), F32),
            vmem((8, 4, 32, 128), BF16),
            vmem((4, 32, 128), BF16),
            vmem((TOK, 32, 128), BF16),
            vmem((TOK * 32, 128), F32),
            vmem((32, D), BF16),
            vmem((1024, 128), BF16),
            vmem((1024, 128), BF16),
            vmem((1024, 128), BF16),
            vmem((1024, 128), BF16),
            vmem((1024, 1024), F32),
            vmem((1024, 128), F32),
            vmem((1024, 128), F32),
            vmem((TOK, HALF, 128), BF16),
            vmem((TOK, HALF, 128), BF16),
            vmem((ROWS, TOK * DH), BF16),
            dma((7,)), dma((64,)), dma((64,)), dma((64,)), dma((64,)),
            dma((8,)), dma, dma((4,)), dma, dma((TOK,)), dma((TOK,)), dma((24,)), dma((24,)),
            dma((8,)), dma((8,)), dma((TOK,)), dma((TOK,)), dma,
        ],
        compiler_params=pltpu.CompilerParams(
            collective_id=0, has_side_effects=True, vmem_limit_bytes=63 * 2**20 + 2**19),
        cost_estimate=pl.CostEstimate(flops=1_200_000_000, bytes_accessed=2_000_000, transcendentals=2_000_000),
        name="cross_frame_attention",
    )(hidden_states, norm_gain, norm_bias, q_weight.T, k_weight.T, v_weight.T, out_weight)


def solution(mesh):
    return jax.shard_map(
        body,
        mesh=mesh,
        in_specs=(P("tm", "tok", None), P(), P(), P(None, "tok"), P(None, "tok"), P(None, "tok"), P("tok", None)),
        out_specs=P("tm", "tok", None),
        check_vma=False,
    )
```

time: 73.4 us -> 61.9 us (0.84)
  the two profiles are of different devices: /device:TPU:19 before, /device:TPU:1 now
where the time goes in v2:
time: 61.9 us; the launch traced here: 61.8 us
  Pallas kernels  60.2 us (97%)
  local copies, waits for them, and re-layouts  1.59 us (3%)
    pallas_call x1, Pallas kernels, body(): pl.pallas_call(kernel, out_shape=jax.ShapeDtypeStruct((1, ROWS, D), BF16)...  60.2 us
    unnamed x1, local copies, waits for them, and re-layouts  1.59 us

profile of v2, /device:TPU:1, one launch (start us, length us, event | category | flops | bytes accessed | tf_op | source)
XLA Modules:
  0.0 61.8 jit_solution(10920241806940863348)
XLA Ops:
  0.0 60.2 %cross_frame_attention.1 = bf16[1,64,1280]{2,1,0:T(8,128)(2,1)} custom-call(bf16[1,64,1280]{2,1,0:T(8,128)(2,1)} %x_hbm.1, f32[1280]{0:T(1024)} %gain_hbm.1, f32[1280]{0:T(1024)} %bias_hbm.1, bf16[64,1280]{1,0:T(8,128)(2,1)} %bitcast.3, bf16[64,1280]{1,0:T(8,128)(2,1)} %bitcast.4, bf16[64,1280]{1,0:T(8,128)(2,1)} %bitcast.5, bf16[64,1280]{1,0:T(8,128)(2,1)} %wo_hbm.1), custom_call_target="tpu_custom_call" | custom-call | flops 1200000000 | bytes 2000000 | tf_op jit(solution)/shard_map/cross_frame_attention/pallas_call | solution.py:449
  60.2 1.6 %copy.9 = bf16[1,64,1280]{2,1,0:T(8,128)(2,1)} copy(bf16[1,64,1280]{2,1,0:T(8,128)(2,1)} %cross_frame_attention.1) | data formatting | bytes 327680

commit v3 on v0

v3 whole, which is shorter than its diff:
```python
import functools
import math

import jax
import jax.numpy as jnp
from jax import lax
from jax.experimental import pallas as pl
from jax.experimental.pallas import tpu as pltpu
from jax.sharding import PartitionSpec as P

MESH = pl.DeviceIdType.MESH
D = 1280
DH = 64
ROWS = 64
HALF = 32
TM = 32
TOK = 16
F32 = jnp.float32
BF16 = jnp.bfloat16
VMEM_LIMIT = 63 * 2**20
EXP_SCALE = DH ** (-0.5) / math.log(2.0)


def layer_norm(states, gain, bias):
    widened = states.astype(F32)
    center = jnp.mean(widened, axis=-1, keepdims=True)
    moved = widened - center
    spread = jnp.mean(jnp.square(moved), axis=-1, keepdims=True)
    return moved * lax.rsqrt(spread + 1e-05) * gain + bias


def kernel(
    x_hbm, gain_hbm, bias_hbm, wq_hbm, wk_hbm, wv_hbm, wo_hbm, o_ref,
    x_in, gain, bias, wall_t,
    wall, xg, wg, kv, keyval, qb, e_first, m_first, l_first, msend, mg, lhs,
    in_sem, tok_send, tok_recv, out_send, out_recv,
    down_send, down_recv, anchor_send, anchor_recv, kv_send, kv_recv, mix_send, mix_recv,
    tok_ready, tm_ready,
):
    tm = lax.axis_index("tm")
    y_lo, z = tm // 8, tm % 8
    me = lax.axis_index("tok")
    y, x, c = me // 8, (me // 2) % 4, me % 2
    xp, xm, xa = (x + 1) % 4, (x + 3) % 4, (x + 2) % 4
    yo, co = 1 - y, 1 - c

    def tid(yy, xx, cc):
        return yy * 8 + xx * 2 + cc

    def each(start, stop, step):
        lax.fori_loop(start, stop, lambda i, carry: (step(i), carry)[1], 0)

    def wait(ref, sem):
        pltpu.make_async_copy(ref, ref, sem).wait()

    def remote(src, dst, send_sem, recv_sem, group, to):
        return pltpu.make_async_remote_copy(
            src_ref=src, dst_ref=dst, send_sem=send_sem, recv_sem=recv_sem,
            device_id=(group, to), device_id_type=MESH)

    for i, src, dst in (
        (0, x_hbm.at[0], x_in), (1, gain_hbm, gain), (2, bias_hbm, bias),
        (3, wk_hbm, wall_t.at[pl.ds(0, DH)]), (3, wv_hbm, wall_t.at[pl.ds(DH, DH)]),
        (3, wq_hbm, wall_t.at[pl.ds(2 * DH, DH)]), (4, wo_hbm, wg.at[me]),
    ):
        pltpu.make_async_copy(src, dst, in_sem.at[i]).start()

    barrier = pltpu.get_barrier_semaphore()

    def greet(group, to):
        pl.semaphore_signal(barrier, inc=1, device_id=(group, to), device_id_type=MESH)

    @pl.when(c == 0)
    def _():
        greet(tm, me + 1)

    @pl.when(c == 1)
    def _():
        greet(tm, me - 1)

    each(1, 8, lambda i: greet(tm, (me + 2 * i) % TOK - c))
    far_side = tid(y, x, 1)
    each(1, 4, lambda i: greet((tm + 8 * i) % TM, far_side))
    each(1, 8, lambda i: greet(y_lo * 8 + (z + i) % 8, far_side))
    greet((tm + 1) % TM, far_side)
    greet((tm + TM - 1) % TM, far_side)

    wait(x_in, in_sem.at[0])
    wait(gain, in_sem.at[1])
    wait(bias, in_sem.at[2])
    normed = layer_norm(x_in[...], gain[...].reshape(1, D), bias[...].reshape(1, D))
    xg[me] = normed.astype(BF16)

    wall_t[3 * DH :] = jnp.zeros((DH, D), BF16)
    wait(wall_t.at[pl.ds(0, 3 * DH)], in_sem.at[3])
    wall[...] = wall_t[...].T
    wait(wg.at[me], in_sem.at[4])

    twin = tid(y, x, co)

    def tell_twin(sem):
        pl.semaphore_signal(sem, inc=1, device_id=(tm, twin), device_id_type=MESH)

    @pl.when(c == 0)
    def _():
        pl.semaphore_wait(barrier, TOK - 1)
        tell_twin(tok_ready)

    @pl.when(c == 1)
    def _():
        pl.semaphore_wait(tok_ready, 1)

    halves = ((0, 32), (32, 32))
    quarters = ((0, 16), (16, 16), (32, 16), (48, 16))
    whole = (0, 64)
    right, left, over = tid(y, xp, c), tid(y, xm, c), tid(yo, x, c)
    row_of, column_of = (y, yo), {"L": xm, "R": xp, "F": xa, "0": x}

    class Gather:
        def __init__(self, buf, send_sem, recv_sem, one_twin):
            self.buf, self.send_sem, self.recv_sem, self.index, self.one_twin = buf, send_sem, recv_sem, {}, one_twin

        def sem(self, *key):
            return self.recv_sem.at[self.index.setdefault(key, len(self.index))]

        def part(self, block, piece):
            return self.buf.at[block, pl.ds(piece[0], piece[1])]

        def send(self, block, piece, to, *key, group=None):
            part = self.part(block, piece)
            remote(part, part, self.send_sem, self.sem(*key), tm if group is None else group, to).start()

        def wait(self, block, piece, *key):
            wait(self.part(block, piece), self.sem(*key))

        def to_twin(self, block, piece, row, place):
            key = ("twin",) if self.one_twin else ("twin", row, place)
            self.send(block, piece, twin, *key)

        def wait_twin(self, row, place):
            self.wait(tid(row_of[row], column_of[place], co), whole, "twin", row, place)

        def own_x(self, piece):
            self.send(me, piece, right, 0, "L", piece)
            self.send(me, piece, left, 0, "R", piece)

        def relay_even(self, row, even):
            from_left, from_right = tid(row_of[row], xm, c), tid(row_of[row], xp, c)
            self.wait(from_left, even, row, "L", even)
            self.send(from_left, even, right, row, "F")
            self.wait(from_right, even, row, "R", even)
            self.to_twin(from_left, even, row, "L")
            self.to_twin(from_right, even, row, "R")

        def relay_odd(self, row, odd):
            from_left, from_right = tid(row_of[row], xm, c), tid(row_of[row], xp, c)
            self.wait(from_right, odd, row, "R", odd)
            self.send(from_right, odd, left, row, "F")
            self.wait(from_left, odd, row, "L", odd)
            self.to_twin(from_left, odd, row, "L")
            self.to_twin(from_right, odd, row, "R")

        def relay(self, row, pieces):
            for even, odd in zip(pieces[::2], pieces[1::2]):
                self.relay_even(row, even)
                self.relay_odd(row, odd)

        def spread_over(self, piece):
            self.send(over, piece, right, 1, "L", piece)
            self.send(over, piece, left, 1, "R", piece)
            self.to_twin(over, piece, 1, "0")

        def far(self, row):
            block = tid(row_of[row], xa, c)
            self.wait(block, whole, row, "F")
            self.to_twin(block, whole, row, "F")

    tok = Gather(xg, tok_send, tok_recv, False)
    out = Gather(wg, out_send, out_recv, True)

    def chip_rows(row, place):
        chip = row_of[row] * 4 + column_of[place]
        return chip, pl.ds(chip * 128, 128)

    def slot(row, place):
        return pl.ds((7 - row * 4 - "0LRF".index(place)) * 128, 128)

    def project(row, place):
        chip, rows = chip_rows(row, place)
        tokens = xg[pl.ds(chip * 2, 2)].reshape(128, D)
        made = jnp.dot(tokens, wall[...], preferred_element_type=F32).astype(BF16)
        kv[rows] = made[:, 0:128]
        qb[rows] = made[:, 128:256]

        @pl.when(tm == 0)
        def _():
            keyval[slot(row, place)] = made[:, 0:128]

    def pass_on(row, place):
        chip, rows = chip_rows(row, place)

        to = 7 - row * 4 - "0LRF".index(place)
        if to > 0:
            @pl.when(tm == 0)
            def _():
                remote(keyval.at[slot(row, place)], keyval.at[slot(row, place)], down_send, down_recv, to, me).start()

        @pl.when((tm < TM - 1) & (tm >= (1 if to == 1 else 0)))
        def _():
            remote(kv.at[rows], keyval.at[pl.ds(1024 + chip * 128, 128)], kv_send, kv_recv,
                   jnp.minimum(tm + 1, TM - 1), me).start()

    def over_in(piece):
        tok.wait(over, piece, "over", piece)
        tok.spread_over(piece)

    part = pl.ds(z * 128, 128)

    def anchor(to, recv):
        remote(keyval.at[part], keyval.at[part], anchor_send, recv, to, me).start()

    def anchor_down():
        for k in (3, 2, 1):
            anchor(k * 8 + z, down_recv)

    def anchor_along():
        def one(to):
            @pl.when((to != z) & (y_lo + to > 0))
            def _():
                anchor(y_lo * 8 + to, anchor_recv)

        each(0, 8, one)

    def own_over(i):
        tok.send(me, quarters[i], over, "over", quarters[i])

    own_over(0)
    tok.own_x(halves[0])
    own_over(1)
    tok.own_x(halves[1])
    own_over(2)
    tok.to_twin(me, whole, 0, "0")
    own_over(3)
    tok.wait_twin(0, "0")
    project(0, "0")

    tok.relay_even(0, halves[0])
    over_in(quarters[0])
    tok.relay_odd(0, halves[1])
    over_in(quarters[1])
    for place in ("L", "R"):
        tok.wait_twin(0, place)
        project(0, place)
    over_in(quarters[2])
    over_in(quarters[3])

    @pl.when(c == 1)
    def _():
        pl.semaphore_wait(barrier, 25)
        tell_twin(tm_ready)

    @pl.when(c == 0)
    def _():
        pl.semaphore_wait(tm_ready, 1)

    for place in ("0", "L", "R"):
        pass_on(0, place)
    mine, theirs = (32 * (z % 2), 32), (32 - 32 * (z % 2), 32)
    out.send(me, mine, over, "over")
    tok.far(0)
    tok.relay(1, quarters[:2])
    tok.wait_twin(0, "F")
    project(0, "F")
    pass_on(0, "F")
    late = z >= 4

    def forward_part():
        wait(keyval.at[part], down_recv)
        anchor_down()
        anchor_along()

    @pl.when((tm < 8) & late)
    def _():
        forward_part()

    tok.relay(1, quarters[2:])
    out.own_x(halves[0])
    out.own_x(halves[1])
    out.to_twin(me, whole, 0, "0")
    for place in ("0", "L", "R"):
        tok.wait_twin(1, place)
        project(1, place)
        pass_on(1, place)
    out.wait(over, mine, "over")
    out.send(over, mine, me, "next", group=tm + 1 - 2 * (z % 2))

    @pl.when((tm > 0) & (tm < 8) & ~late)
    def _():
        forward_part()

    @pl.when((tm >= 8) & late)
    def _():
        wait(keyval.at[part], down_recv)
        anchor_along()

    tok.far(1)
    tok.wait_twin(1, "F")
    project(1, "F")
    pass_on(1, "F")
    out.relay(0, halves)

    @pl.when(tm == 0)
    def _():
        keyval[1024:2048] = kv[...]
        anchor_down()
        anchor_along()

    @pl.when((tm >= 8) & ~late)
    def _():
        wait(keyval.at[part], down_recv)
        anchor_along()

    out.wait(over, theirs, "next")
    for half in halves:
        out.spread_over(half)

    anchor_first = z == 0
    first_keys = pl.ds(jnp.where(anchor_first, 0, 1024), 1024)
    second_keys = pl.ds(jnp.where(anchor_first, 1024, 0), 1024)

    def wait_anchor():
        wait(keyval.at[pl.ds(0, 7 * 128)], anchor_recv)

    def wait_prev():
        @pl.when(tm == 1)
        def _():
            wait(keyval.at[pl.ds(1024, 7 * 128)], kv_recv)
            keyval[pl.ds(1024 + chip_rows(1, "R")[0] * 128, 128)] = keyval[slot(1, "R")]

        @pl.when(tm > 1)
        def _():
            wait(keyval.at[pl.ds(1024, 1024)], kv_recv)

    @pl.when(anchor_first & (tm > 0))
    def _():
        wait_anchor()

    @pl.when(z > 0)
    def _():
        wait_prev()

    low = lax.broadcasted_iota(jnp.int32, (HALF, 128), 1) < DH
    nt = (((1,), (1,)), ((), ()))

    def chunk(i):
        yy = (y + 1 + i // 2) % 2
        pp = (x // 2 + 1 + i) % 2
        return yy * 8 + pp * 4

    def attend_first(i):
        rows = pl.ds(chunk(i) * ROWS, 4 * ROWS)
        scores = lax.dot_general(qb[rows], keyval[first_keys], nt, preferred_element_type=F32)
        highest = jnp.max(scores, axis=-1, keepdims=True)
        weights = jnp.exp2((scores - highest) * EXP_SCALE)
        e_first[rows] = weights
        m_first[rows] = jnp.broadcast_to(highest, (4 * ROWS, 128))
        l_first[rows] = jnp.broadcast_to(jnp.sum(weights, axis=-1, keepdims=True), (4 * ROWS, 128))

    def attend(i):
        first = chunk(i)
        rows = pl.ds(first * ROWS, 4 * ROWS)
        scores = lax.dot_general(qb[rows], keyval[second_keys], nt, preferred_element_type=F32)
        before = m_first[rows][:, 0:1]
        highest = jnp.maximum(jnp.max(scores, axis=-1, keepdims=True), before)
        weights = jnp.exp2((scores - highest) * EXP_SCALE)
        shrink = jnp.exp2((before - highest) * EXP_SCALE)
        inverse = 1.0 / (jnp.sum(weights, axis=-1, keepdims=True) + l_first[rows][:, 0:1] * shrink)
        p_second = (weights * inverse).astype(BF16)
        p_first = (e_first[rows] * (shrink * inverse)).astype(BF16)
        mixed = jnp.dot(p_second, keyval[second_keys], preferred_element_type=F32)
        mixed = mixed + jnp.dot(p_first, keyval[first_keys], preferred_element_type=F32)
        for k in range(4):
            top = mixed[k * ROWS : k * ROWS + HALF]
            bottom = mixed[k * ROWS + HALF : (k + 1) * ROWS]
            to = first + k
            msend[to] = jnp.where(low, pltpu.roll(top, DH, 1), bottom).astype(BF16)

            @pl.when(to != me)
            def _():
                remote(msend.at[to], mg.at[me], mix_send, mix_recv, tm, to).start()

    each(0, 4, attend_first)
    out.relay(1, halves)
    out.far(0)

    @pl.when(anchor_first & (tm > 0))
    def _():
        wait_prev()

    @pl.when(z > 0)
    def _():
        wait_anchor()

    each(0, 4, attend)
    out.far(1)
    mg[me] = msend[me]

    wait(xg.at[pl.ds(0, 15)], tok_send)

    @pl.when(tm == 0)
    def _():
        wait(kv.at[pl.ds(0, 7 * 128)], down_send)
        wait(keyval.at[pl.ds(0, 10 * 128)], anchor_send)

    @pl.when((tm > 0) & (tm < 8))
    def _():
        wait(keyval.at[pl.ds(0, 9 * 128)], anchor_send)

    @pl.when(tm >= 8)
    def _():
        wait(keyval.at[pl.ds(0, 7 * 128)], anchor_send)

    @pl.when(tm == 0)
    def _():
        wait(kv.at[pl.ds(0, 7 * 128)], kv_send)

    @pl.when((tm > 0) & (tm < TM - 1))
    def _():
        wait(kv, kv_send)

    wait(mg.at[pl.ds(0, TOK - 1)], mix_recv)
    for i in range(8):
        even = mg[2 * i].astype(F32)
        odd = mg[2 * i + 1].astype(F32)
        lhs[0:HALF, i * 128 : (i + 1) * 128] = jnp.where(low, even, pltpu.roll(odd, DH, 1)).astype(BF16)
        lhs[HALF:ROWS, i * 128 : (i + 1) * 128] = jnp.where(low, pltpu.roll(even, DH, 1), odd).astype(BF16)
    wait(wg.at[pl.ds(0, 8)], out.sem("twin"))
    o_ref[0] = jnp.dot(lhs[...], wg[...].reshape(TOK * DH, D), preferred_element_type=F32).astype(BF16)
    wait(wg.at[pl.ds(0, 15)], out_send)
    wait(msend.at[pl.ds(0, TOK - 1)], mix_send)


def body(hidden_states, norm_gain, norm_bias, q_weight, k_weight, v_weight, out_weight):
    anywhere = pl.BlockSpec(memory_space=pltpu.HBM)
    vmem = pltpu.VMEM
    dma = pltpu.SemaphoreType.DMA
    return pl.pallas_call(
        kernel,
        out_shape=jax.ShapeDtypeStruct((1, ROWS, D), BF16),
        in_specs=[anywhere] * 7,
        out_specs=pl.BlockSpec(memory_space=pltpu.VMEM),
        scratch_shapes=[
            vmem((ROWS, D), BF16), vmem((D,), F32), vmem((D,), F32),
            vmem((256, D), BF16),
            vmem((D, 256), BF16),
            vmem((TOK, ROWS, D), BF16),
            vmem((TOK, ROWS, D), BF16),
            vmem((1024, 128), BF16),
            vmem((2048, 128), BF16),
            vmem((1024, 128), BF16),
            vmem((1024, 1024), F32),
            vmem((1024, 128), F32),
            vmem((1024, 128), F32),
            vmem((TOK, HALF, 128), BF16),
            vmem((TOK, HALF, 128), BF16),
            vmem((ROWS, TOK * DH), BF16),
            dma((5,)), dma, dma((26,)), dma, dma((13,)),
            dma, dma, dma, dma, dma, dma, dma, dma,
            pltpu.SemaphoreType.REGULAR, pltpu.SemaphoreType.REGULAR,
        ],
        compiler_params=pltpu.CompilerParams(
            collective_id=0, has_side_effects=True, vmem_limit_bytes=VMEM_LIMIT),
        cost_estimate=pl.CostEstimate(flops=1_200_000_000, bytes_accessed=2_000_000, transcendentals=2_000_000),
        name="cross_frame_attention",
    )(hidden_states, norm_gain, norm_bias, q_weight.T, k_weight.T, v_weight.T, out_weight)


def solution(mesh):
    return jax.shard_map(
        body,
        mesh=mesh,
        in_specs=(P("tm", "tok", None), P(), P(), P(None, "tok"), P(None, "tok"), P(None, "tok"), P("tok", None)),
        out_specs=P("tm", "tok", None),
        check_vma=False,
    )
```

time: 549 us -> 57.2 us (0.10)
  the two profiles are of different devices: /device:TPU:1 before, /device:TPU:11 now
where the time goes in v3:
time: 57.2 us; the launch traced here: 57 us
  Pallas kernels  55.4 us (97%)
  local copies, waits for them, and re-layouts  1.59 us (3%)
    pallas_call x1, Pallas kernels, body(): pl.pallas_call(kernel, out_shape=jax.ShapeDtypeStruct((1, ROWS, D), BF16)...  55.4 us
    unnamed x1, local copies, waits for them, and re-layouts  1.59 us

profile of v3, /device:TPU:11, one launch (start us, length us, event | category | flops | bytes accessed | tf_op | source)
XLA Modules:
  0.0 57.0 jit_solution(1003898729047350312)
XLA Ops:
  0.0 55.4 %cross_frame_attention.1 = bf16[1,64,1280]{2,1,0:T(8,128)(2,1)} custom-call(bf16[1,64,1280]{2,1,0:T(8,128)(2,1)} %x_hbm.1, f32[1280]{0:T(1024)} %gain_hbm.1, f32[1280]{0:T(1024)} %bias_hbm.1, bf16[64,1280]{1,0:T(8,128)(2,1)} %bitcast.3, bf16[64,1280]{1,0:T(8,128)(2,1)} %bitcast.4, bf16[64,1280]{1,0:T(8,128)(2,1)} %bitcast.5, bf16[64,1280]{1,0:T(8,128)(2,1)} %wo_hbm.1), custom_call_target="tpu_custom_call" | custom-call | flops 1200000000 | bytes 2000000 | tf_op jit(solution)/shard_map/cross_frame_attention/pallas_call | solution.py:447
  55.4 1.6 %copy.9 = bf16[1,64,1280]{2,1,0:T(8,128)(2,1)} copy(bf16[1,64,1280]{2,1,0:T(8,128)(2,1)} %cross_frame_attention.1) | data formatting | bytes 327680

commit v4 on v3

--- a/solution.py
+++ b/solution.py
@@ -32,9 +32,9 @@
 def kernel(
     x_hbm, gain_hbm, bias_hbm, wq_hbm, wk_hbm, wv_hbm, wo_hbm, o_ref,
     x_in, gain, bias, wall_t,
-    wall, xg, wg, kv, keyval, qb, e_first, m_first, l_first, msend, mg, lhs,
+    wall, xg, wg, kv, keyval, qb, e_first, m_first, l_first, e_second, m_second, l_second, msend, mg, lhs, partial,
     in_sem, tok_send, tok_recv, out_send, out_recv,
-    down_send, down_recv, anchor_send, anchor_recv, kv_send, kv_recv, mix_send, mix_recv,
+    down_send, down_recv, anchor_send, anchor_recv, kv_send, kv_recv, mix_out, mix_near, mix_far,
     tok_ready, tm_ready,
 ):
     tm = lax.axis_index("tm")
@@ -205,7 +205,7 @@
             def _():
                 remote(keyval.at[slot(row, place)], keyval.at[slot(row, place)], down_send, down_recv, to, me).start()
 
-        @pl.when((tm < TM - 1) & (tm >= (1 if to == 1 else 0)))
+        @pl.when((tm > 0) & (tm < TM - 1))
         def _():
             remote(kv.at[rows], keyval.at[pl.ds(1024 + chip * 128, 128)], kv_send, kv_recv,
                    jnp.minimum(tm + 1, TM - 1), me).start()
@@ -265,21 +265,35 @@
 
     for place in ("0", "L", "R"):
         pass_on(0, place)
-    mine, theirs = (32 * (z % 2), 32), (32 - 32 * (z % 2), 32)
-    out.send(me, mine, over, "over")
+    late, last = z >= 4, z >= 5
+
+    def forward_part():
+        wait(keyval.at[part], down_recv)
+        anchor_down()
+        anchor_along()
+
+    def forward_along():
+        wait(keyval.at[part], down_recv)
+        anchor_along()
+
+    def own_over_out():
+        for half in halves:
+            out.send(me, half, over, "over", half)
+
+    @pl.when(~last)
+    def _():
+        own_over_out()
+
+    @pl.when((tm < 8) & last)
+    def _():
+        forward_part()
+
     tok.far(0)
     tok.relay(1, quarters[:2])
     tok.wait_twin(0, "F")
     project(0, "F")
     pass_on(0, "F")
-    late = z >= 4
-
-    def forward_part():
-        wait(keyval.at[part], down_recv)
-        anchor_down()
-        anchor_along()
-
-    @pl.when((tm < 8) & late)
+    @pl.when(tm == 4)
     def _():
         forward_part()
 
@@ -291,22 +305,19 @@
         tok.wait_twin(1, place)
         project(1, place)
         pass_on(1, place)
-    out.wait(over, mine, "over")
-    out.send(over, mine, me, "next", group=tm + 1 - 2 * (z % 2))
-
     @pl.when((tm > 0) & (tm < 8) & ~late)
     def _():
         forward_part()
-
-    @pl.when((tm >= 8) & late)
-    def _():
-        wait(keyval.at[part], down_recv)
-        anchor_along()
 
     tok.far(1)
     tok.wait_twin(1, "F")
     project(1, "F")
     pass_on(1, "F")
+
+    @pl.when(last)
+    def _():
+        own_over_out()
+
     out.relay(0, halves)
 
     @pl.when(tm == 0)
@@ -315,93 +326,73 @@
         anchor_down()
         anchor_along()
 
-    @pl.when((tm >= 8) & ~late)
-    def _():
-        wait(keyval.at[part], down_recv)
-        anchor_along()
-
-    out.wait(over, theirs, "next")
+    @pl.when(tm >= 8)
+    def _():
+        forward_along()
+
     for half in halves:
+        out.wait(over, half, "over", half)
         out.spread_over(half)
 
-    anchor_first = z == 0
-    first_keys = pl.ds(jnp.where(anchor_first, 0, 1024), 1024)
-    second_keys = pl.ds(jnp.where(anchor_first, 1024, 0), 1024)
+    first_keys, second_keys = slice(1024, 2048), slice(0, 1024)
 
     def wait_anchor():
         wait(keyval.at[pl.ds(0, 7 * 128)], anchor_recv)
 
-    def wait_prev():
-        @pl.when(tm == 1)
-        def _():
-            wait(keyval.at[pl.ds(1024, 7 * 128)], kv_recv)
-            keyval[pl.ds(1024 + chip_rows(1, "R")[0] * 128, 128)] = keyval[slot(1, "R")]
-
-        @pl.when(tm > 1)
-        def _():
-            wait(keyval.at[pl.ds(1024, 1024)], kv_recv)
-
-    @pl.when(anchor_first & (tm > 0))
+    @pl.when(tm == 1)
     def _():
         wait_anchor()
-
-    @pl.when(z > 0)
-    def _():
-        wait_prev()
+        keyval[1024:2048] = keyval[0:1024]
+
+    @pl.when(tm > 1)
+    def _():
+        wait(keyval.at[pl.ds(1024, 1024)], kv_recv)
 
     low = lax.broadcasted_iota(jnp.int32, (HALF, 128), 1) < DH
     nt = (((1,), (1,)), ((), ()))
 
-    def chunk(i):
-        yy = (y + 1 + i // 2) % 2
-        pp = (x // 2 + 1 + i) % 2
-        return yy * 8 + pp * 4
-
-    def attend_first(i):
-        rows = pl.ds(chunk(i) * ROWS, 4 * ROWS)
-        scores = lax.dot_general(qb[rows], keyval[first_keys], nt, preferred_element_type=F32)
+    def weigh(rows, count, keys, weights_ref, highest_ref, total_ref):
+        scores = lax.dot_general(qb[rows], keyval[keys], nt, preferred_element_type=F32)
         highest = jnp.max(scores, axis=-1, keepdims=True)
         weights = jnp.exp2((scores - highest) * EXP_SCALE)
-        e_first[rows] = weights
-        m_first[rows] = jnp.broadcast_to(highest, (4 * ROWS, 128))
-        l_first[rows] = jnp.broadcast_to(jnp.sum(weights, axis=-1, keepdims=True), (4 * ROWS, 128))
-
-    def attend(i):
-        first = chunk(i)
-        rows = pl.ds(first * ROWS, 4 * ROWS)
-        scores = lax.dot_general(qb[rows], keyval[second_keys], nt, preferred_element_type=F32)
-        before = m_first[rows][:, 0:1]
-        highest = jnp.maximum(jnp.max(scores, axis=-1, keepdims=True), before)
-        weights = jnp.exp2((scores - highest) * EXP_SCALE)
-        shrink = jnp.exp2((before - highest) * EXP_SCALE)
-        inverse = 1.0 / (jnp.sum(weights, axis=-1, keepdims=True) + l_first[rows][:, 0:1] * shrink)
-        p_second = (weights * inverse).astype(BF16)
-        p_first = (e_first[rows] * (shrink * inverse)).astype(BF16)
-        mixed = jnp.dot(p_second, keyval[second_keys], preferred_element_type=F32)
-        mixed = mixed + jnp.dot(p_first, keyval[first_keys], preferred_element_type=F32)
-        for k in range(4):
+        weights_ref[rows] = weights
+        highest_ref[rows] = jnp.broadcast_to(highest, (count, 128))
+        total_ref[rows] = jnp.broadcast_to(jnp.sum(weights, axis=-1, keepdims=True), (count, 128))
+
+    def mix(first, count):
+        rows = pl.ds(first * ROWS, count * ROWS)
+        top_first, top_second = m_first[rows][:, 0:1], m_second[rows][:, 0:1]
+        highest = jnp.maximum(top_first, top_second)
+        shrink_first = jnp.exp2((top_first - highest) * EXP_SCALE)
+        shrink_second = jnp.exp2((top_second - highest) * EXP_SCALE)
+        inverse = 1.0 / (l_first[rows][:, 0:1] * shrink_first + l_second[rows][:, 0:1] * shrink_second)
+        p_first = (e_first[rows] * (shrink_first * inverse)).astype(BF16)
+        p_second = (e_second[rows] * (shrink_second * inverse)).astype(BF16)
+        mixed = jnp.dot(p_first, keyval[first_keys], preferred_element_type=F32)
+        mixed = mixed + jnp.dot(p_second, keyval[second_keys], preferred_element_type=F32)
+        for k in range(count):
             top = mixed[k * ROWS : k * ROWS + HALF]
             bottom = mixed[k * ROWS + HALF : (k + 1) * ROWS]
-            to = first + k
-            msend[to] = jnp.where(low, pltpu.roll(top, DH, 1), bottom).astype(BF16)
-
-            @pl.when(to != me)
-            def _():
-                remote(msend.at[to], mg.at[me], mix_send, mix_recv, tm, to).start()
-
-    each(0, 4, attend_first)
+            msend[first + k] = jnp.where(low, pltpu.roll(top, DH, 1), bottom).astype(BF16)
+
+    def mix_send(to, near):
+        remote(msend.at[to], mg.at[me], mix_out, mix_near if near else mix_far, tm, to).start()
+
+    weigh(slice(0, 1024), 1024, first_keys, e_first, m_first, l_first)
     out.relay(1, halves)
     out.far(0)
 
-    @pl.when(anchor_first & (tm > 0))
-    def _():
-        wait_prev()
-
-    @pl.when(z > 0)
+    @pl.when(tm > 1)
     def _():
         wait_anchor()
 
-    each(0, 4, attend)
+    for yy in (yo, y):
+        weigh(pl.ds(yy * 8 * ROWS, 8 * ROWS), 8 * ROWS, second_keys, e_second, m_second, l_second)
+        for quad in (0, 4):
+            mix(yy * 8 + quad, 4)
+            if yy is yo:
+                each(quad, quad + 4, lambda k: mix_send(yo * 8 + k, False))
+    each(1, 8, lambda k: mix_send(y * 8 + (me + k) % 8, True))
     out.far(1)
     mg[me] = msend[me]
 
@@ -409,7 +400,7 @@
 
     @pl.when(tm == 0)
     def _():
-        wait(kv.at[pl.ds(0, 7 * 128)], down_send)
+        wait(keyval.at[pl.ds(0, 7 * 128)], down_send)
         wait(keyval.at[pl.ds(0, 10 * 128)], anchor_send)
 
     @pl.when((tm > 0) & (tm < 8))
@@ -420,24 +411,26 @@
     def _():
         wait(keyval.at[pl.ds(0, 7 * 128)], anchor_send)
 
-    @pl.when(tm == 0)
-    def _():
-        wait(kv.at[pl.ds(0, 7 * 128)], kv_send)
-
     @pl.when((tm > 0) & (tm < TM - 1))
     def _():
         wait(kv, kv_send)
 
-    wait(mg.at[pl.ds(0, TOK - 1)], mix_recv)
-    for i in range(8):
-        even = mg[2 * i].astype(F32)
-        odd = mg[2 * i + 1].astype(F32)
-        lhs[0:HALF, i * 128 : (i + 1) * 128] = jnp.where(low, even, pltpu.roll(odd, DH, 1)).astype(BF16)
-        lhs[HALF:ROWS, i * 128 : (i + 1) * 128] = jnp.where(low, pltpu.roll(even, DH, 1), odd).astype(BF16)
+    def gathered(yy):
+        for i in range(4):
+            even = mg[yy * 8 + 2 * i].astype(F32)
+            odd = mg[yy * 8 + 2 * i + 1].astype(F32)
+            lhs[0:HALF, i * 128 : (i + 1) * 128] = jnp.where(low, even, pltpu.roll(odd, DH, 1)).astype(BF16)
+            lhs[HALF:ROWS, i * 128 : (i + 1) * 128] = jnp.where(low, pltpu.roll(even, DH, 1), odd).astype(BF16)
+        weights = wg[pl.ds(yy * 8, 8)].reshape(8 * DH, D)
+        return jnp.dot(lhs[...], weights, preferred_element_type=F32)
+
     wait(wg.at[pl.ds(0, 8)], out.sem("twin"))
-    o_ref[0] = jnp.dot(lhs[...], wg[...].reshape(TOK * DH, D), preferred_element_type=F32).astype(BF16)
+    wait(mg.at[pl.ds(0, 7)], mix_near)
+    partial[...] = gathered(y)
+    wait(mg.at[pl.ds(0, 8)], mix_far)
+    o_ref[0] = (partial[...] + gathered(yo)).astype(BF16)
     wait(wg.at[pl.ds(0, 15)], out_send)
-    wait(msend.at[pl.ds(0, TOK - 1)], mix_send)
+    wait(msend.at[pl.ds(0, TOK - 1)], mix_out)
 
 
 def body(hidden_states, norm_gain, norm_bias, q_weight, k_weight, v_weight, out_weight):
@@ -461,11 +454,15 @@
             vmem((1024, 1024), F32),
             vmem((1024, 128), F32),
             vmem((1024, 128), F32),
+            vmem((1024, 1024), F32),
+            vmem((1024, 128), F32),
+            vmem((1024, 128), F32),
             vmem((TOK, HALF, 128), BF16),
             vmem((TOK, HALF, 128), BF16),
-            vmem((ROWS, TOK * DH), BF16),
+            vmem((ROWS, 8 * DH), BF16),
+            vmem((ROWS, D), F32),
             dma((5,)), dma, dma((26,)), dma, dma((13,)),
-            dma, dma, dma, dma, dma, dma, dma, dma,
+            dma, dma, dma, dma, dma, dma, dma, dma, dma,
             pltpu.SemaphoreType.REGULAR, pltpu.SemaphoreType.REGULAR,
         ],
         compiler_params=pltpu.CompilerParams(

time: 57.2 us -> 54.9 us (0.960)
  the two profiles are of different devices: /device:TPU:11 before, /device:TPU:9 now
where the time goes in v4:
time: 54.9 us; the launch traced here: 54.7 us
  Pallas kernels  53.1 us (97%)
  local copies, waits for them, and re-layouts  1.59 us (3%)
    pallas_call x1, Pallas kernels, body(): pl.pallas_call(kernel, out_shape=jax.ShapeDtypeStruct((1, ROWS, D), BF16)...  53.1 us
    unnamed x1, local copies, waits for them, and re-layouts  1.59 us

profile of v4, /device:TPU:9, one launch (start us, length us, event | category | flops | bytes accessed | tf_op | source)
XLA Modules:
  0.0 54.7 jit_solution(17129245666551301397)
XLA Ops:
  0.0 53.1 %cross_frame_attention.1 = bf16[1,64,1280]{2,1,0:T(8,128)(2,1)} custom-call(bf16[1,64,1280]{2,1,0:T(8,128)(2,1)} %x_hbm.1, f32[1280]{0:T(1024)} %gain_hbm.1, f32[1280]{0:T(1024)} %bias_hbm.1, bf16[64,1280]{1,0:T(8,128)(2,1)} %bitcast.3, bf16[64,1280]{1,0:T(8,128)(2,1)} %bitcast.4, bf16[64,1280]{1,0:T(8,128)(2,1)} %bitcast.5, bf16[64,1280]{1,0:T(8,128)(2,1)} %wo_hbm.1), custom_call_target="tpu_custom_call" | custom-call | flops 1200000000 | bytes 2000000 | tf_op jit(solution)/shard_map/cross_frame_attention/pallas_call | solution.py:440
  53.1 1.6 %copy.9 = bf16[1,64,1280]{2,1,0:T(8,128)(2,1)} copy(bf16[1,64,1280]{2,1,0:T(8,128)(2,1)} %cross_frame_attention.1) | data formatting | bytes 327680

commit v5 on v4

--- a/solution.py
+++ b/solution.py
@@ -17,7 +17,7 @@
 TOK = 16
 F32 = jnp.float32
 BF16 = jnp.bfloat16
-VMEM_LIMIT = 63 * 2**20
+VMEM_LIMIT = 53 * 2**20 + 2**19 + 16 * 2**14
 EXP_SCALE = DH ** (-0.5) / math.log(2.0)
 
 
@@ -314,6 +314,10 @@
     project(1, "F")
     pass_on(1, "F")
 
+    @pl.when((tm >= 8) & last)
+    def _():
+        forward_along()
+
     @pl.when(last)
     def _():
         own_over_out()
@@ -326,7 +330,7 @@
         anchor_down()
         anchor_along()
 
-    @pl.when(tm >= 8)
+    @pl.when((tm >= 8) & ~last)
     def _():
         forward_along()
 

time: 54.9 us -> 54.6 us (level)
  Pallas kernels: 53.1 us -> 52.3 us
    pallas_call x1, Pallas kernels: 53.1 us -> 52.3 us  [body(): pl.pallas_call(kernel, out_shape=jax.ShapeDtypeStruct((1, ROWS, D), BF16)...]
    unnamed x1 -> x5, local copies, waits for them, and re-layouts: 1.59 us -> 2.06 us
where the time goes in v5:
time: 54.6 us; the launch traced here: 54.4 us
  Pallas kernels  52.3 us (96%)
  local copies, waits for them, and re-layouts  2.06 us (4%)
    pallas_call x1, Pallas kernels, body(): pl.pallas_call(kernel, out_shape=jax.ShapeDtypeStruct((1, ROWS, D), BF16)...  52.3 us
    unnamed x5, local copies, waits for them, and re-layouts  2.06 us

profile of v5, /device:TPU:9, one launch (start us, length us, event | category | flops | bytes accessed | tf_op | source)
XLA Modules:
  0.0 54.4 jit_solution(8559188954653798893)
XLA Ops:
  0.0 0.0 copy-start
  0.0 0.7 %copy-done = f32[1280]{0:T(1024)S(1)} copy-done((f32[1280]{0:T(1024)S(1)}, f32[1280]{0:T(1024)}, u32[]{:S(2)}) %copy-start) | copy-done | bytes 5144
  0.7 0.0 copy-start.1
  0.7 0.7 %copy-done.1 = f32[1280]{0:T(1024)S(1)} copy-done((f32[1280]{0:T(1024)S(1)}, f32[1280]{0:T(1024)}, u32[]{:S(2)}) %copy-start.1) | copy-done | bytes 5144
  1.4 52.3 %cross_frame_attention.1 = bf16[1,64,1280]{2,1,0:T(8,128)(2,1)S(1)} custom-call(bf16[1,64,1280]{2,1,0:T(8,128)(2,1)} %x_hbm.1, f32[1280]{0:T(1024)S(1)} %copy-done, f32[1280]{0:T(1024)S(1)} %copy-done.1, bf16[64,1280]{1,0:T(8,128)(2,1)} %bitcast.3, bf16[64,1280]{1,0:T(8,128)(2,1)} %bitcast.4, bf16[64,1280]{1,0:T(8,128)(2,1)} %bitcast.5, bf16[64,1280]{1,0:T(8,128)(2,1)} %wo_hbm.1), custom_call_target="tpu_custom_call" | custom-call | flops 1200000000 | bytes 2000000 | tf_op jit(solution)/shard_map/cross_frame_attention/pallas_call | solution.py:444
  53.7 0.7 %copy.9 = bf16[1,64,1280]{2,1,0:T(8,128)(2,1)} copy(bf16[1,64,1280]{2,1,0:T(8,128)(2,1)S(1)} %cross_frame_attention.1) | data formatting | bytes 327680
Async XLA Ops:
  0.0 0.7 %copy-start = (f32[1280]{0:T(1024)S(1)}, f32[1280]{0:T(1024)}, u32[]{:S(2)}) copy-start(f32[1280]{0:T(1024)} %gain_hbm.1) | copy-start | bytes 15364
  0.7 0.7 %copy-start.1 = (f32[1280]{0:T(1024)S(1)}, f32[1280]{0:T(1024)}, u32[]{:S(2)}) copy-start(f32[1280]{0:T(1024)} %bias_hbm.1) | copy-start | bytes 15364

commit v6 on v5

--- a/solution.py
+++ b/solution.py
@@ -382,6 +382,11 @@
     def mix_send(to, near):
         remote(msend.at[to], mg.at[me], mix_out, mix_near if near else mix_far, tm, to).start()
 
+    def near_send(k):
+        @pl.when(y * 8 + k != me)
+        def _():
+            mix_send(y * 8 + k, True)
+
     weigh(slice(0, 1024), 1024, first_keys, e_first, m_first, l_first)
     out.relay(1, halves)
     out.far(0)
@@ -396,7 +401,8 @@
             mix(yy * 8 + quad, 4)
             if yy is yo:
                 each(quad, quad + 4, lambda k: mix_send(yo * 8 + k, False))
-    each(1, 8, lambda k: mix_send(y * 8 + (me + k) % 8, True))
+            else:
+                each(quad, quad + 4, near_send)
     out.far(1)
     mg[me] = msend[me]
 

time: 54.6 us -> 54 us (0.989)
  Pallas kernels: 52.3 us -> 51.7 us
    pallas_call x1, Pallas kernels: 52.3 us -> 51.7 us  [body(): pl.pallas_call(kernel, out_shape=jax.ShapeDtypeStruct((1, ROWS, D), BF16)...]
where the time goes in v6:
time: 54 us; the launch traced here: 53.8 us
  Pallas kernels  51.7 us (96%)
  local copies, waits for them, and re-layouts  2.06 us (4%)
    pallas_call x1, Pallas kernels, body(): pl.pallas_call(kernel, out_shape=jax.ShapeDtypeStruct((1, ROWS, D), BF16)...  51.7 us
    unnamed x5, local copies, waits for them, and re-layouts  2.06 us

profile of v6, /device:TPU:9, one launch (start us, length us, event | category | flops | bytes accessed | tf_op | source)
XLA Modules:
  0.0 53.8 jit_solution(4358481842461972969)
XLA Ops:
  0.0 0.0 copy-start
  0.0 0.7 %copy-done = f32[1280]{0:T(1024)S(1)} copy-done((f32[1280]{0:T(1024)S(1)}, f32[1280]{0:T(1024)}, u32[]{:S(2)}) %copy-start) | copy-done | bytes 5144
  0.7 0.0 copy-start.1
  0.7 0.7 %copy-done.1 = f32[1280]{0:T(1024)S(1)} copy-done((f32[1280]{0:T(1024)S(1)}, f32[1280]{0:T(1024)}, u32[]{:S(2)}) %copy-start.1) | copy-done | bytes 5144
  1.4 51.7 %cross_frame_attention.1 = bf16[1,64,1280]{2,1,0:T(8,128)(2,1)S(1)} custom-call(bf16[1,64,1280]{2,1,0:T(8,128)(2,1)} %x_hbm.1, f32[1280]{0:T(1024)S(1)} %copy-done, f32[1280]{0:T(1024)S(1)} %copy-done.1, bf16[64,1280]{1,0:T(8,128)(2,1)} %bitcast.3, bf16[64,1280]{1,0:T(8,128)(2,1)} %bitcast.4, bf16[64,1280]{1,0:T(8,128)(2,1)} %bitcast.5, bf16[64,1280]{1,0:T(8,128)(2,1)} %wo_hbm.1), custom_call_target="tpu_custom_call" | custom-call | flops 1200000000 | bytes 2000000 | tf_op jit(solution)/shard_map/cross_frame_attention/pallas_call | solution.py:450
  53.1 0.7 %copy.9 = bf16[1,64,1280]{2,1,0:T(8,128)(2,1)} copy(bf16[1,64,1280]{2,1,0:T(8,128)(2,1)S(1)} %cross_frame_attention.1) | data formatting | bytes 327680
Async XLA Ops:
  0.0 0.7 %copy-start = (f32[1280]{0:T(1024)S(1)}, f32[1280]{0:T(1024)}, u32[]{:S(2)}) copy-start(f32[1280]{0:T(1024)} %gain_hbm.1) | copy-start | bytes 15364
  0.7 0.7 %copy-start.1 = (f32[1280]{0:T(1024)S(1)}, f32[1280]{0:T(1024)}, u32[]{:S(2)}) copy-start(f32[1280]{0:T(1024)} %bias_hbm.1) | copy-start | bytes 15364
